TPU v7x, 32 devices: a whole 2x2x4 slice. The times are simulated.
32 devices in a mesh: crop: 4 (over y, x), chan: 8 (over z, core).
Axes of the slice: x: 2, y: 2, z: 4, core: 2. Of those that a mesh axis runs over, the one named last changes fastest.
Arguments:
- features: bfloat16 [4, 2048, 1024], P('crop', 'chan'), may hold values from -6 to 6
- low_in: bfloat16 [4, 256, 128, 128], P('crop', 'chan'), may hold values from -6 to 6
- offsets: int32 [4, 2], P('crop'), may hold values from 0 to 1791, as said below
- d_logits: bfloat16 [4, 21, 128, 128], P('crop'), may hold values from -6 to 6
- w_point: bfloat16 [2048, 256], P('chan'), may hold values from -0.125 to 0.125
- w_atrous: bfloat16 [3, 9, 2048, 256], P(None, None, 'chan'), may hold values from -0.046875 to 0.046875
- w_pool: bfloat16 [2048, 256], P('chan'), may hold values from -0.125 to 0.125
- w_proj: bfloat16 [5, 256, 256], P(None, 'chan'), may hold values from -0.15625 to 0.15625
- w_low: bfloat16 [256, 48], P('chan'), may hold values from -0.375 to 0.375
- w_dec1: bfloat16 [9, 256, 256], P(None, 'chan'), may hold values from -0.109375 to 0.109375
- w_dec1_low: bfloat16 [9, 48, 256], P(None, None, 'chan'), may hold values from -0.109375 to 0.109375
- w_dec2: bfloat16 [9, 256, 256], P(None, 'chan'), may hold values from -0.125 to 0.125
- w_cls: bfloat16 [256, 21], P('chan'), may hold values from -0.375 to 0.375
- b_cls: float32 [21], replicated, may hold values from -3 to 3
- bn_gain: float32 [8, 256], P(None, 'chan'), may hold values from 0.1 to 1.9
- bn_shift: float32 [8, 256], P(None, 'chan'), may hold values from -3 to 3
- low_gain: float32 [48], replicated, may hold values from 0.1 to 1.9
- low_shift: float32 [48], replicated, may hold values from -3 to 3
Outputs:
- logits: float32 [4, 21, 128, 128], P('crop', None, 'chan')
- d_features: float32 [4, 2048, 1024], P('crop', 'chan')
- d_low_in: float32 [4, 256, 128, 128], P('crop', 'chan')
- d_w_point: float32 [2048, 256], P('chan')
- d_w_atrous: float32 [3, 9, 2048, 256], P(None, None, 'chan')
- d_w_pool: float32 [2048, 256], P('chan')
- d_w_proj: float32 [5, 256, 256], P(None, 'chan')
- d_w_low: float32 [256, 48], P('chan')
- d_w_dec1: float32 [9, 256, 256], P(None, 'chan')
- d_w_dec1_low: float32 [9, 48, 256], P(None, None, 'chan')
- d_w_dec2: float32 [9, 256, 256], P(None, 'chan')
- d_w_cls: float32 [256, 21], P('chan')
- d_b_cls: float32 [21], replicated
- d_bn_gain: float32 [8, 256], P(None, 'chan')
- d_bn_shift: float32 [8, 256], P(None, 'chan')
- d_low_gain: float32 [48], replicated
- d_low_shift: float32 [48], replicated
Inputs may be any that keep to these rules, and one draw needn't show every extreme that they name: offsets[:, 0] is below 768 and offsets[:, 1] below 1792; some crop's column is the largest allowed.
All inputs are finite; a program needn't handle non-finite values.
Results may differ from a plain program's by a relative error of at most 0.02.
The roundings to bfloat16 on the way count: a program that leaves them out, or rounds other values in their place, can miss the bound.
Values may be sent and summed in bfloat16 or wider, within the bound.
A program may use at most 320 MiB of HBM per device.

v0:
```python
import jax
import jax.numpy as jnp
from jax import lax
from jax.sharding import PartitionSpec as P

FA = 32
SCENE_H = 1024
SCENE_W = 2048


epsilon = 1e-05
highest = lax.Precision.HIGHEST
atrous_rates = (6, 12, 18)


def shifted(values, step_down, across):
    height = values.shape[-2]
    breadth = values.shape[-1]
    pad_rows = abs(step_down)
    pad_cols = abs(across)
    padded = jnp.pad(values, ((0, 0), (0, 0), (pad_rows, pad_rows), (pad_cols, pad_cols)))
    return padded[
        :,
        :,
        pad_rows + step_down : pad_rows + step_down + height,
        pad_cols + across : pad_cols + across + breadth,
    ]


def conv_rows(inputs, weight, dilation):
    result = None
    for position in range(9):
        step_down = (position // 3 - 1) * dilation
        across = (position % 3 - 1) * dilation
        tap_term = jnp.einsum(
            "cbhw,co->obhw",
            shifted(inputs, step_down, across),
            weight[position],
            preferred_element_type=jnp.float32,
        )
        result = tap_term if result is None else result + tap_term
    return result


def conv_back_input(gradient, weight, dilation):
    result = None
    for position in range(9):
        step_down = (position // 3 - 1) * dilation
        across = (position % 3 - 1) * dilation
        tap_term = jnp.einsum(
            "obhw,co->cbhw", gradient, weight[position], preferred_element_type=jnp.float32
        )
        tap_term = shifted(tap_term, -step_down, -across)
        result = tap_term if result is None else result + tap_term
    return result


def conv_back_weight(inputs, gradient, dilation):
    pieces = []
    for position in range(9):
        step_down = (position // 3 - 1) * dilation
        across = (position % 3 - 1) * dilation
        pieces.append(
            jnp.einsum(
                "cbhw,obhw->co",
                shifted(inputs, step_down, across),
                gradient,
                preferred_element_type=jnp.float32,
            )
        )
    return jnp.stack(pieces, axis=0)


def reduce_channels(build_rows, own_rows):
    return lax.psum_scatter(
        build_rows(jnp.int32(0), own_rows * lax.axis_size("chan")),
        "chan",
        scatter_dimension=0,
        tiled=True,
    )


def gather_grads(values):
    return lax.all_gather(values, "chan", axis=0, tiled=True)


def channel_total(values):
    return lax.psum(values, "chan")


def channel_share(values):
    return lax.psum_scatter(values, "chan", scatter_dimension=0, tiled=True)


def row_share(values):
    return lax.psum_scatter(values, "chan", scatter_dimension=2, tiled=True)


def norm_forward(values, scales, shifts):
    samples = values.shape[-1] * lax.axis_size("crop")
    summed = jnp.sum(values, axis=-1)
    squares = jnp.sum(values * values, axis=-1)
    summed, squares = lax.psum((summed, squares), "crop")
    average = summed / samples
    inverse = lax.rsqrt(squares / samples - average * average + epsilon)
    normed = (values - average[..., None]) * inverse[..., None]
    before = scales[..., None] * normed + shifts[..., None]
    return (jax.nn.gelu(before), (normed, inverse, before))


def norm_backward(incoming, saved, scales):
    normed, inverse, before = saved
    pushed = jax.vjp(jax.nn.gelu, before)[1](incoming)[0]
    samples = pushed.shape[-1] * lax.axis_size("crop")
    summed = jnp.sum(pushed, axis=-1)
    along = jnp.sum(pushed * normed, axis=-1)
    summed, along = lax.psum((summed, along), "crop")
    result = (scales * inverse)[..., None] * (
        pushed - (summed / samples)[..., None] - normed * (along / samples)[..., None]
    )
    return (result, along, summed)


def conv_forward(inputs, weight, own_rows):

    def build_rows(first_row, row_count):
        return conv_rows(inputs, weight, 1)

    return reduce_channels(build_rows, own_rows)


def conv_backward(gradient, inputs, weight):
    full_grads = gather_grads(gradient)
    return (conv_back_input(full_grads, weight, 1), conv_back_weight(inputs, full_grads, 1))


def per_device(
    features,
    low_in,
    offsets,
    d_logits,
    w_point,
    w_atrous,
    w_pool,
    w_proj,
    w_low,
    w_dec1,
    w_dec1_low,
    w_dec2,
    w_cls,
    b_cls,
    bn_gain,
    bn_shift,
    low_gain,
    low_shift,
):
    crop_count = features.shape[0]
    grid_side = FA
    fine_side = low_in.shape[2]
    c_own = w_dec2.shape[1]
    low_width = w_low.shape[1]
    bf16 = jnp.bfloat16
    f32 = jnp.float32
    row_count = fine_side // lax.axis_size("chan")
    row_start = lax.axis_index("chan") * row_count
    row_index = jnp.arange(fine_side, dtype=jnp.int32)
    rows_valid = offsets[:, 0:1] + 4 * row_index[None, :] < SCENE_H
    cols_valid = offsets[:, 1:2] + 4 * row_index[None, :] < SCENE_W
    valid_mask = (rows_valid[:, :, None] & cols_valid[:, None, :]).astype(f32)
    row_mask = lax.dynamic_slice_in_dim(valid_mask, row_start, row_count, 1)
    source_pos = jnp.clip(
        (jnp.arange(fine_side, dtype=f32) + 0.5) / 4.0 - 0.5, 0.0, grid_side - 1.0
    )
    coarse_cols = jnp.arange(grid_side, dtype=f32)[None, :]
    up_table = jnp.maximum(0.0, 1.0 - jnp.abs(source_pos[:, None] - coarse_cols))
    source = features.reshape(crop_count, features.shape[1], grid_side, grid_side).transpose(
        1, 0, 2, 3
    )
    early_maps = low_in.transpose(1, 0, 2, 3)

    def aspp_build(first_row, row_total):
        branch_parts = [jnp.einsum("cbhw,co->obhw", source, w_point, preferred_element_type=f32)]
        for branch_no in range(3):
            branch_parts.append(conv_rows(source, w_atrous[branch_no], atrous_rates[branch_no]))
        return jnp.stack(branch_parts, axis=1)

    branch_pre = reduce_channels(aspp_build, c_own)
    aspp_gains = bn_gain[0:4].T
    branch_act, branch_saved = norm_forward(
        branch_pre.reshape(c_own, 4, -1), aspp_gains, bn_shift[0:4].T
    )
    branch_low = branch_act.astype(bf16).reshape(c_own, 4, crop_count, grid_side, grid_side)
    pooled = jnp.mean(source.astype(f32), axis=(2, 3)).astype(bf16)
    pool_terms = jnp.einsum("cb,co->ob", pooled, w_pool, preferred_element_type=f32)
    pool_pre = channel_share(pool_terms)
    pool_act, pool_saved = norm_forward(pool_pre, bn_gain[4], bn_shift[4])
    pool_low = pool_act.astype(bf16)

    def proj_build(first_row, row_total):
        spatial = jnp.einsum("ckbhw,kco->obhw", branch_low, w_proj[0:4], preferred_element_type=f32)
        pooled_part = jnp.einsum("cb,co->ob", pool_low, w_proj[4], preferred_element_type=f32)
        return spatial + pooled_part[:, :, None, None]

    projected = reduce_channels(proj_build, c_own)
    merged, merged_saved = norm_forward(projected.reshape(c_own, -1), bn_gain[5], bn_shift[5])
    merged = merged.reshape(c_own, crop_count, grid_side, grid_side)
    masked_grad = (d_logits * valid_mask[:, None].astype(bf16)).transpose(1, 0, 2, 3)
    cls_bias_grad = jnp.sum(masked_grad.astype(f32), axis=(1, 2, 3))
    low_terms = jnp.einsum("cbhw,co->obhw", early_maps, w_low, preferred_element_type=f32)
    upsampled = jnp.einsum(
        "cbhw,ih,jw->cbij", merged, up_table, up_table, precision=highest
    ).astype(bf16)
    low_pre = channel_total(low_terms)
    low_act, low_saved = norm_forward(low_pre.reshape(low_width, -1), low_gain, low_shift)
    low_bf = low_act.astype(bf16).reshape(low_width, crop_count, fine_side, fine_side)
    side_part = conv_rows(low_bf, w_dec1_low, 1)
    dec1_pre = conv_forward(upsampled, w_dec1, c_own)
    first_act, first_saved = norm_forward(
        (dec1_pre + side_part).reshape(c_own, -1), bn_gain[6], bn_shift[6]
    )
    first_bf = first_act.astype(bf16).reshape(c_own, crop_count, fine_side, fine_side)
    dec2_pre = conv_forward(first_bf, w_dec2, c_own)
    second_act, second_saved = norm_forward(dec2_pre.reshape(c_own, -1), bn_gain[7], bn_shift[7])
    second_bf = second_act.astype(bf16).reshape(c_own, crop_count, fine_side, fine_side)
    logit_terms = jnp.einsum("cbhw,co->obhw", second_bf, w_cls, preferred_element_type=f32)
    logit_rows = row_share(logit_terms)
    logits = (logit_rows + b_cls[:, None, None, None]) * row_mask[None]
    cls_weight_grad = jnp.einsum(
        "cbhw,obhw->co", second_bf, masked_grad, preferred_element_type=f32
    )
    second_grad = jnp.einsum("obhw,co->cbhw", masked_grad, w_cls, preferred_element_type=f32)
    dec2_grad, gain_seven, shift_seven = norm_backward(
        second_grad.reshape(c_own, -1), second_saved, bn_gain[7]
    )
    dec2_bf = dec2_grad.astype(bf16).reshape(c_own, crop_count, fine_side, fine_side)
    first_grad, dec2_wgrad = conv_backward(dec2_bf, first_bf, w_dec2)
    dec1_grad, gain_six, shift_six = norm_backward(
        first_grad.reshape(c_own, -1), first_saved, bn_gain[6]
    )
    dec1_bf = dec1_grad.astype(bf16).reshape(c_own, crop_count, fine_side, fine_side)
    up_grad, dec1_wgrad = conv_backward(dec1_bf, upsampled, w_dec1)
    side_partial = conv_back_input(dec1_bf, w_dec1_low, 1)
    low_act_grad = channel_total(side_partial)
    side_wgrad = conv_back_weight(low_bf, dec1_bf, 1)
    low_pre_grad, low_gain_grad, low_shift_grad = norm_backward(
        low_act_grad.reshape(low_width, -1), low_saved, low_gain
    )
    low_pre_bf = low_pre_grad.astype(bf16).reshape(low_width, crop_count, fine_side, fine_side)
    low_wgrad = jnp.einsum("cbhw,obhw->co", early_maps, low_pre_bf, preferred_element_type=f32)
    early_grad = jnp.einsum("obhw,co->cbhw", low_pre_bf, w_low, preferred_element_type=f32)
    merged_grad = jnp.einsum("cbij,ih,jw->cbhw", up_grad, up_table, up_table, precision=highest)
    proj_grad, gain_five, shift_five = norm_backward(
        merged_grad.reshape(c_own, -1), merged_saved, bn_gain[5]
    )
    proj_bf = proj_grad.astype(bf16).reshape(c_own, crop_count, grid_side, grid_side)
    proj_full = gather_grads(proj_bf)
    branch_act_grad = jnp.einsum(
        "obhw,kco->ckbhw", proj_full, w_proj[0:4], preferred_element_type=f32
    )
    proj_sums = jnp.sum(proj_full.astype(f32), axis=(2, 3))
    pool_act_grad = jnp.einsum("co,ob->cb", w_proj[4].astype(f32), proj_sums, precision=highest)
    proj_wgrad_spatial = jnp.einsum(
        "ckbhw,obhw->kco", branch_low, proj_full, preferred_element_type=f32
    )
    proj_wgrad_pool = jnp.einsum("cb,ob->co", pool_low.astype(f32), proj_sums, precision=highest)
    proj_wgrad = jnp.concatenate([proj_wgrad_spatial, proj_wgrad_pool[None]], axis=0)
    branch_grad, gains_aspp, shifts_aspp = norm_backward(
        branch_act_grad.reshape(c_own, 4, -1), branch_saved, aspp_gains
    )
    pool_grad, gain_four, shift_four = norm_backward(pool_act_grad, pool_saved, bn_gain[4])
    branch_bf = branch_grad.astype(bf16).reshape(c_own, 4, crop_count, grid_side, grid_side)
    pool_bf = pool_grad.astype(bf16)
    branch_full, pool_full = (
        lax.all_gather(branch_bf, "chan", axis=0, tiled=True),
        lax.all_gather(pool_bf, "chan", axis=0, tiled=True),
    )
    point_grad = branch_full[:, 0]
    source_grad = jnp.einsum("obhw,co->cbhw", point_grad, w_point, preferred_element_type=f32)
    point_wgrad = jnp.einsum("cbhw,obhw->co", source, point_grad, preferred_element_type=f32)
    atrous_pieces = []
    for branch_no in range(3):
        atrous_grad = branch_full[:, branch_no + 1]
        source_grad = source_grad + conv_back_input(
            atrous_grad, w_atrous[branch_no], atrous_rates[branch_no]
        )
        atrous_pieces.append(conv_back_weight(source, atrous_grad, atrous_rates[branch_no]))
    atrous_wgrad = jnp.stack(atrous_pieces, axis=0)
    pooled_grad = jnp.einsum("ob,co->cb", pool_full, w_pool, preferred_element_type=f32)
    source_grad = source_grad + pooled_grad[:, :, None, None] / (grid_side * grid_side)
    pool_wgrad = jnp.einsum("cb,ob->co", pooled, pool_full, preferred_element_type=f32)
    (
        point_wgrad,
        atrous_wgrad,
        pool_wgrad,
        proj_wgrad,
        low_wgrad,
        dec1_wgrad,
        side_wgrad,
        dec2_wgrad,
        cls_weight_grad,
        cls_bias_grad,
    ) = lax.psum(
        (
            point_wgrad,
            atrous_wgrad,
            pool_wgrad,
            proj_wgrad,
            low_wgrad,
            dec1_wgrad,
            side_wgrad,
            dec2_wgrad,
            cls_weight_grad,
            cls_bias_grad,
        ),
        "crop",
    )
    gain_grad = jnp.concatenate(
        [gains_aspp.T, jnp.stack([gain_four, gain_five, gain_six, gain_seven], axis=0)], axis=0
    )
    shift_grad = jnp.concatenate(
        [shifts_aspp.T, jnp.stack([shift_four, shift_five, shift_six, shift_seven], axis=0)], axis=0
    )
    feature_grad = source_grad.transpose(1, 0, 2, 3).reshape(
        crop_count, source_grad.shape[0], grid_side * grid_side
    )
    return (
        logits.transpose(1, 0, 2, 3),
        feature_grad,
        early_grad.transpose(1, 0, 2, 3),
        point_wgrad,
        atrous_wgrad,
        pool_wgrad,
        proj_wgrad,
        low_wgrad,
        dec1_wgrad,
        side_wgrad,
        dec2_wgrad,
        cls_weight_grad,
        cls_bias_grad,
        gain_grad,
        shift_grad,
        low_gain_grad,
        low_shift_grad,
    )


def solution(mesh):
    placed = (
        P("crop", "chan", None),
        P("crop", "chan", None, None),
        P("crop", None),
        P("crop", None, None, None),
        P("chan", None),
        P(None, None, "chan", None),
        P("chan", None),
        P(None, "chan", None),
        P("chan", None),
        P(None, "chan", None),
        P(None, None, "chan"),
        P(None, "chan", None),
        P("chan", None),
        P(),
        P(None, "chan"),
        P(None, "chan"),
        P(),
        P(),
    )
    return jax.shard_map(
        per_device,
        mesh=mesh,
        in_specs=placed,
        out_specs=(
            P("crop", None, "chan", None),
            P("crop", "chan", None),
            P("crop", "chan", None, None),
            P("chan", None),
            P(None, None, "chan", None),
            P("chan", None),
            P(None, "chan", None),
            P("chan", None),
            P(None, "chan", None),
            P(None, None, "chan"),
            P(None, "chan", None),
            P("chan", None),
            P(),
            P(None, "chan"),
            P(None, "chan"),
            P(),
            P(),
        ),
        check_vma=False,
    )
```

profile of v0, /device:TPU:0, one launch (start us, length us, event | category | flops | bytes accessed | tf_op | source)
XLA Modules:
  0.0 1790.2 jit_solution(7936190363495164243)
XLA Ops:
  36.4 7.5 reduce-scatter.21.cloned.1.call-done
  44.7 49.8 %reduce-scatter.19.cloned.1.call-done = f32[32,4096]{1,0:T(8,128)} async-done(((f32[256,4096]{1,0:T(8,128)}), f32[32,4096]{1,0:T(8,128)}) %reduce-scatter.19.cloned.1.call-update) | async-done | bytes 524304
  96.5 10.0 all-reduce.74
  113.7 59.0 %all-reduce.80.cloned.1.call-done = f32[48,1,128,128]{3,0,2,1:T(8,128)} async-done(((f32[48,1,128,128]{3,0,2,1:T(8,128)}), f32[48,1,128,128]{3,0,2,1:T(8,128)}) %all-reduce.80.cloned.1.call-update) | async-done | bytes 3145744 | tf_op jit(solution)/shard_map/psum | solution.py:88
  175.1 32.6 %reduce-scatter.23.cloned.1.call-done = f32[32,1024]{1,0:T(8,128)} async-done(((f32[256,1024]{1,0:T(8,128)}), f32[32,1024]{1,0:T(8,128)}) %reduce-scatter.23.cloned.1.call-update) | async-done | bytes 131088
  208.9 9.8 all-reduce.73
  227.6 8.2 fusion.491
  235.8 8.3 fusion.494
  244.0 8.2 fusion.497
  252.2 8.2 fusion.503
  260.4 8.5 fusion.506
  268.9 8.2 fusion.509
  277.2 8.3 fusion.512
  285.5 8.2 fusion.500
  293.7 47.7 %add_bitcast_fusion.1 = f32[256,1,128,128]{0,3,2,1:T(8,128)} fusion(f32[128,128,256]{2,1,0:T(8,128)} %fusion.491, f32[128,128,256]{2,1,0:T(8,128)} %fusion.494, f32[128,128,256]{2,1,0:T(8,128)} %fusion.497, f32[128,128,256]{2,1,0:T(8,128)} %fusion.500, f32[128,128,256]{2,1,0:T(8,128)} %fusion.503, f32[128,128,256]{2,1,0:T(8,128)} %fusion.506, ...), kind=kOutput, calls=%fused_computation.1 | convolution fusion | flops 301989888 | bytes 152059904 | tf_op jit(solution)/shard_map/cbhw,co->obhw/dot_general | solution.py:35
  341.4 18.1 %copy.309 = f32[256,1,128,128]{3,2,1,0:T(8,128)} copy(f32[256,1,128,128]{0,3,2,1:T(8,128)} %add_bitcast_fusion.1) | data formatting | bytes 33554432 | tf_op jit(solution)/shard_map/add | solution.py:41
  379.9 144.4 %reduce-scatter.13.cloned.1.call-done = f32[32,1,128,128]{3,2,1,0:T(8,128)} async-done(((f32[256,1,128,128]{3,2,1,0:T(8,128)}), f32[32,1,128,128]{3,2,1,0:T(8,128)}) %reduce-scatter.13.cloned.1.call-update) | async-done | bytes 2097168 | tf_op jit(solution)/shard_map/reduce_scatter | solution.py:75
  524.3 10.1 fusion.1078
  534.4 10.4 all-reduce.72
  547.5 8.1 fusion.459
  555.6 8.2 fusion.462
  563.8 8.1 fusion.465
  571.9 9.6 fusion.518
  581.5 9.8 fusion.521
  591.2 9.7 fusion.526
  600.9 9.7 fusion.529
  610.5 9.7 fusion.532
  620.2 47.7 %add_bitcast_fusion = f32[256,1,128,128]{0,3,2,1:T(8,128)} fusion(f32[128,128,256]{2,1,0:T(8,128)} %fusion.459, f32[128,128,256]{2,1,0:T(8,128)} %fusion.526, f32[128,128,256]{2,1,0:T(8,128)} %fusion.518, f32[128,128,256]{2,1,0:T(8,128)} %fusion.462, f32[128,128,256]{2,1,0:T(8,128)} %fusion.521, f32[128,128,256]{2,1,0:T(8,128)} %fusion.529, ...), kind=kOutput, calls=%fused_computation | convolution fusion | flops 301989888 | bytes 152059904 | tf_op jit(solution)/shard_map/cbhw,co->obhw/dot_general | solution.py:35
  667.9 18.1 %copy.312 = f32[256,1,128,128]{3,2,1,0:T(8,128)} copy(f32[256,1,128,128]{0,3,2,1:T(8,128)} %add_bitcast_fusion) | data formatting | bytes 33554432 | tf_op jit(solution)/shard_map/add | solution.py:41
  689.5 161.4 %reduce-scatter.15.cloned.1.call-done = f32[32,1,128,128]{3,2,1,0:T(8,128)} async-done(((f32[256,1,128,128]{3,2,1,0:T(8,128)}), f32[32,1,128,128]{3,2,1,0:T(8,128)}) %reduce-scatter.15.cloned.1.call-update) | async-done | bytes 2097168 | tf_op jit(solution)/shard_map/reduce_scatter | solution.py:75
  852.9 9.8 all-reduce.71
  870.1 8.0 all-reduce.70
  885.3 79.2 %all-gather.4.cloned.1.call-done = bf16[256,1,128,128]{3,2,1,0:T(8,128)(2,1)} async-done(((bf16[32,1,128,128]{3,2,1,0:T(8,128)(2,1)}), bf16[256,1,128,128]{3,2,1,0:T(8,128)(2,1)}) %all-gather.4.cloned.1.call-update) | async-done | bytes 8388624 | tf_op jit(solution)/shard_map/all_gather | solution.py:84
  964.5 8.4 fusion.146
  1011.6 21.5 %fusion.1075 = (f32[32]{0:T(128)S(1)}, f32[32]{0:T(128)S(1)}, f32[32,1,128,128]{3,0,2,1:T(8,128)}) fusion(f32[32]{0:T(128)S(1)} %get-tuple-element.162, f32[32,1,128,128]{3,0,2,1:T(8,128)S(1)} %copy-done.15, f32[32]{0:T(128)S(1)} %get-tuple-element.161, f32[32]{0:T(128)S(1)} %get-tuple-element.152, f32[32]{0:T(128)S(1)} %get-tuple-element.174, ...), kind=kOutput, calls=%fused_computation.1192 | convolution fusion | flops 286261184 | bytes 29378816 | tf_op jit(solution)/shard_map/obhw,co->cbhw/dot_general | solution.py:50
  1033.2 10.1 all-reduce.69
  1051.6 7.1 fusion.79
  1071.3 61.1 %all-reduce.82.cloned.1.call-done = f32[48,1,128,128]{3,0,2,1:T(8,128)} async-done(((f32[48,1,128,128]{3,0,2,1:T(8,128)}), f32[48,1,128,128]{3,0,2,1:T(8,128)}) %all-reduce.82.cloned.1.call-update) | async-done | bytes 3145744 | tf_op jit(solution)/shard_map/psum | solution.py:88
  1139.0 77.1 %all-gather.6.cloned.1.call-done = bf16[256,1,128,128]{3,2,1,0:T(8,128)(2,1)} async-done(((bf16[32,1,128,128]{3,2,1,0:T(8,128)(2,1)}), bf16[256,1,128,128]{3,2,1,0:T(8,128)(2,1)}) %all-gather.6.cloned.1.call-update) | async-done | bytes 8388624 | tf_op jit(solution)/shard_map/all_gather | solution.py:84
  1216.1 8.4 fusion.172
  1260.5 21.0 %fusion.102 = f32[32,128,128]{2,0,1:T(8,128)} fusion(f32[32,1,128,128]{3,0,2,1:T(8,128)S(1)} %fusion.192, f32[32,1,128,128]{3,0,2,1:T(8,128)S(1)} %fusion.175, f32[32,1,128,128]{3,0,2,1:T(8,128)S(1)} %fusion.186, f32[32,1,128,128]{3,0,2,1:T(8,128)S(1)} %fusion.181, f32[32,1,128,128]{3,0,2,1:T(8,128)} %fusion.195, f32[32,1,128,128]{3,0,2,1:T(8,128)S(1)} %fusion.189, ...), kind=kOutput, calls=%fused_computation.189 | convolution fusion | flops 272629760 | bytes 27279360 | tf_op jit(solution)/shard_map/obhw,co->cbhw/dot_general | solution.py:50
  1288.0 10.4 all-reduce.68
  1299.5 20.8 %all_gather.17 = bf16[256,1,32,32]{3,2,1,0:T(8,128)(2,1)S(1)} all-gather(bf16[32,1,32,32]{3,2,1,0:T(8,128)(2,1)S(1)} %copy.322), channel_id=1, replica_groups=mesh['crop'=4,'chan'=8] {'chan'}, dimensions={0}, use_global_device_ids=true | all-gather | bytes 589824 | tf_op jit(solution)/shard_map/all_gather | solution.py:84
  1333.3 18.5 %all-reduce.67 = (f32[32,4]{0,1:T(4,128)S(1)}, f32[32,4]{0,1:T(4,128)S(1)}, f32[32]{0:T(128)S(1)}, f32[32]{0:T(128)S(1)}, f32[32,48]{1,0:T(8,128)}, /*index=5*/f...) all-reduce(f32[32,4]{0,1:T(4,128)S(1)} %get-tuple-element.73, ...), channel_id=1, replica_groups=mesh['crop'=4,'chan'=8] {'crop'}, use_global_device_ids=true, to_apply=%region_45.46 | all-reduce | flops 16373 | bytes 130984 | tf_op jit(solution)/shard_map/psum | solution.py:117
  1361.9 12.0 fusion.288
  1373.9 12.1 fusion.294
  1386.1 12.2 fusion.300
  1398.4 8.4 fusion.306
  1406.8 8.8 fusion.312
  1415.7 8.6 fusion.318
  1424.3 8.7 fusion.324
  1432.9 8.4 fusion.330
  1441.4 8.9 fusion.336
  1452.6 13.8 all-reduce.66
  1467.8 12.2 fusion.342
  1480.0 12.4 fusion.348
  1492.5 12.6 fusion.354
  1505.2 8.8 fusion.360
  1514.0 8.7 fusion.366
  1522.7 8.9 fusion.372
  1531.6 9.1 fusion.378
  1540.7 9.1 fusion.384
  1549.9 8.6 fusion.390
  1623.4 148.1 %all-reduce.84.cloned.1.call-done = (f32[256,256]{0,1:T(8,128)}, f32[3,9,256,256]{3,2,1,0:T(8,128)}, f32[256,256]{1,0:T(8,128)}, f32[5,32,256]{2,1,0:T(8,128)}, ...) async-done(((f32[256,256]{0,1:T(8,128)}, f32[3,9,256,256]{3,2,1,0:T(8,128)}, f32[256,256]{1,0:T(8,128)}, f32[5,32,256]{2,1,0:T(8,128)}, f32[9,32,256]{2,1,0:T(8,128)}, ...) | async-done | bytes 8355856 | tf_op jit(solution)/shard_map/psum | solution.py:302
  (557 shorter events, 305.2 us)
Async XLA Ops:
  7.2 25.4 %copy-start = (bf16[1,32,128,128]{3,2,1,0:T(8,128)(2,1)S(1)}, bf16[1,32,128,128]{3,2,1,0:T(8,128)(2,1)}, u32[]{:S(2)}) copy-start(bf16[1,32,128,128]{3,2,1,0:T(8,128)(2,1)} %param.19) | copy-start | bytes 3145732
  7.2 36.7 %reduce-scatter.21.cloned.1.call-start = ((), (), s32[]{:S(2)}) async-start(), calls=%async_computation.15 | async-start | bytes 147456
  10.9 83.6 %reduce-scatter.19.cloned.1.call-start = ((), (), s32[]{:S(2)}) async-start(), calls=%async_computation.14 | async-start | bytes 4718592
  12.2 11.4 copy-start.3
  32.6 140.1 %all-reduce.80.cloned.1.call-start = ((), (), s32[]{:S(2)}) async-start(), calls=%async_computation.7 | async-start | bytes 6291456 | tf_op jit(solution)/shard_map/psum | solution.py:88
  35.7 171.9 %reduce-scatter.23.cloned.1.call-start = ((), (), s32[]{:S(2)}) async-start(), calls=%async_computation.16 | async-start | bytes 1179648
  36.4 71.4 %copy-start.114 = (f32[32,4]{0,1:T(4,128)}, f32[32,4]{0,1:T(4,128)S(1)}, u32[]{:S(2)}) copy-start(f32[32,4]{0,1:T(4,128)S(1)} %get-tuple-element.172) | copy-start | bytes 1540
  36.4 71.4 %copy-start.116 = (f32[32,4]{0,1:T(4,128)}, f32[32,4]{0,1:T(4,128)S(1)}, u32[]{:S(2)}) copy-start(f32[32,4]{0,1:T(4,128)S(1)} %get-tuple-element.173) | copy-start | bytes 1540
  44.7 62.9 %copy-start.142 = (bf16[5,32,256]{2,1,0:T(8,128)(2,1)S(1)}, bf16[5,32,256]{2,1,0:T(8,128)(2,1)}, u32[]{:S(2)}) copy-start(bf16[5,32,256]{2,1,0:T(8,128)(2,1)} %param.25) | copy-start | bytes 245764
  96.2 14.1 copy-start.11
  112.8 411.4 %reduce-scatter.13.cloned.1.call-start = ((), (), s32[]{:S(2)}) async-start(), calls=%async_computation.6 | async-start | bytes 18874368 | tf_op jit(solution)/shard_map/reduce_scatter | solution.py:75
  113.1 107.6 %copy-start.91 = (f32[128]{0:T(128)}, f32[128]{0:T(128)S(1)}, u32[]{:S(2)}) copy-start(f32[128]{0:T(128)S(1)} %add_clamp_fusion) | copy-start | bytes 1540
  113.7 105.9 %copy-start.99 = (f32[32]{0:T(128)}, f32[32]{0:T(128)S(1)}, u32[]{:S(2)}) copy-start(f32[32]{0:T(128)S(1)} %get-tuple-element.151) | copy-start | bytes 388
  113.7 106.0 %copy-start.101 = (f32[32]{0:T(128)}, f32[32]{0:T(128)S(1)}, u32[]{:S(2)}) copy-start(f32[32]{0:T(128)S(1)} %get-tuple-element.175) | copy-start | bytes 388
  208.8 15.4 copy-start.21
  224.2 61.2 %copy-start.19 = (bf16[128,32,128]{2,0,1:T(8,128)(2,1)}, bf16[128,32,128]{2,0,1:T(8,128)(2,1)S(1)}, u32[]{:S(2)}) copy-start(bf16[128,32,128]{2,0,1:T(8,128)(2,1)S(1)} %convolution_convert_fusion) | copy-start | bytes 3145732
  227.5 16.5 copy-start.30
  227.5 24.7 %copy-start.32 = (bf16[32,128,128]{2,1,0:T(8,128)(2,1)}, bf16[32,128,128]{2,1,0:T(8,128)(2,1)S(1)}, u32[]{:S(2)}) copy-start(bf16[32,128,128]{2,1,0:T(8,128)(2,1)S(1)} %get-tuple-element.139) | copy-start | bytes 3145732
  227.5 32.9 %copy-start.34 = (bf16[32,128,128]{2,1,0:T(8,128)(2,1)}, bf16[32,128,128]{2,1,0:T(8,128)(2,1)S(1)}, u32[]{:S(2)}) copy-start(bf16[32,128,128]{2,1,0:T(8,128)(2,1)S(1)} %get-tuple-element.137) | copy-start | bytes 3145732
  227.5 41.4 %copy-start.36 = (bf16[32,128,128]{2,1,0:T(8,128)(2,1)}, bf16[32,128,128]{2,1,0:T(8,128)(2,1)S(1)}, u32[]{:S(2)}) copy-start(bf16[32,128,128]{2,1,0:T(8,128)(2,1)S(1)} %get-tuple-element.140) | copy-start | bytes 3145732
  227.6 49.6 %copy-start.38 = (bf16[32,128,128]{2,1,0:T(8,128)(2,1)}, bf16[32,128,128]{2,1,0:T(8,128)(2,1)S(1)}, u32[]{:S(2)}) copy-start(bf16[32,128,128]{2,1,0:T(8,128)(2,1)S(1)} %get-tuple-element.141) | copy-start | bytes 3145732
  227.6 66.1 %copy-start.24 = (bf16[32,128,128]{2,1,0:T(8,128)(2,1)}, bf16[32,128,128]{2,1,0:T(8,128)(2,1)S(1)}, u32[]{:S(2)}) copy-start(bf16[32,128,128]{2,1,0:T(8,128)(2,1)S(1)} %get-tuple-element.134) | copy-start | bytes 3145732
  359.5 491.4 %reduce-scatter.15.cloned.1.call-start = ((), (), s32[]{:S(2)}) async-start(), calls=%async_computation.8 | async-start | bytes 18874368 | tf_op jit(solution)/shard_map/reduce_scatter | solution.py:75
  364.8 159.5 %copy-start.5 = (bf16[48,1,128,128]{3,0,2,1:T(8,128)(2,1)}, bf16[48,1,128,128]{3,0,2,1:T(8,128)(2,1)S(1)}, u32[]{:S(2)}) copy-start(bf16[48,1,128,128]{3,0,2,1:T(8,128)(2,1)S(1)} %multiply_convert_fusion.1) | copy-start | bytes 4718596
  534.4 13.0 copy-start.49
  547.4 72.8 %copy-start.9 = (bf16[32,1,128,128]{3,0,2,1:T(8,128)(2,1)}, bf16[32,1,128,128]{3,0,2,1:T(8,128)(2,1)S(1)}, u32[]{:S(2)}) copy-start(bf16[32,1,128,128]{3,0,2,1:T(8,128)(2,1)S(1)} %multiply_convert_fusion.5) | copy-start | bytes 3145732
  686.0 176.8 %copy-start.110 = (f32[32]{0:T(128)S(1)}, f32[32]{0:T(128)}, u32[]{:S(2)}) copy-start(f32[32]{0:T(128)} %copy-done.109) | copy-start | bytes 388
  686.0 176.8 %copy-start.112 = (f32[32]{0:T(128)S(1)}, f32[32]{0:T(128)}, u32[]{:S(2)}) copy-start(f32[32]{0:T(128)} %copy-done.111) | copy-start | bytes 388
  686.0 178.1 %copy-start.81 = (bf16[32,21]{0,1:T(8,128)(2,1)S(1)}, bf16[32,21]{0,1:T(8,128)(2,1)}, u32[]{:S(2)}) copy-start(bf16[32,21]{0,1:T(8,128)(2,1)} %param.30) | copy-start | bytes 4036
  686.0 178.1 %copy-start.103 = (f32[32]{0:T(128)S(1)}, f32[32]{0:T(128)}, u32[]{:S(2)}) copy-start(f32[32]{0:T(128)} %get-tuple-element.150) | copy-start | bytes 388
  686.0 178.1 %copy-start.104 = (f32[32]{0:T(128)S(1)}, f32[32]{0:T(128)}, u32[]{:S(2)}) copy-start(f32[32]{0:T(128)} %get-tuple-element.176) | copy-start | bytes 388
  686.0 278.5 %all-gather.4.cloned.1.call-start = ((), (), s32[]{:S(2)}) async-start(), calls=%async_computation.10 | async-start | bytes 9437184 | tf_op jit(solution)/shard_map/all_gather | solution.py:84
  688.5 174.2 %copy-start.105 = (pred[128]{0:T(512)(128)(4,1)}, pred[128]{0:T(512)(128)(4,1)S(1)}, u32[]{:S(2)}) copy-start(pred[128]{0:T(512)(128)(4,1)S(1)} %get-tuple-element.178) | copy-start | bytes 388
  688.5 181.6 %copy-start.89 = (pred[128]{0:T(512)(128)(4,1)}, pred[128]{0:T(512)(128)(4,1)S(1)}, u32[]{:S(2)}) copy-start(pred[128]{0:T(512)(128)(4,1)S(1)} %get-tuple-element.177) | copy-start | bytes 388
  864.1 14.6 copy-start.23
  884.8 247.6 %all-reduce.82.cloned.1.call-start = ((), (), s32[]{:S(2)}) async-start(), calls=%async_computation.13 | async-start | bytes 6291456 | tf_op jit(solution)/shard_map/psum | solution.py:88
  1058.7 157.4 %all-gather.6.cloned.1.call-start = ((), (), s32[]{:S(2)}) async-start(), calls=%async_computation.11 | async-start | bytes 9437184 | tf_op jit(solution)/shard_map/all_gather | solution.py:84
  1061.6 496.9 %all-gather.8.cloned.1.call-start = ((), (), s32[]{:S(2)}) async-start(), calls=%async_computation.12 | async-start | bytes 9437184 | tf_op jit(solution)/shard_map/all_gather | solution.py:274
  1070.0 62.4 %copy-start.67 = (f32[48]{0:T(128)S(1)}, f32[48]{0:T(128)}, u32[]{:S(2)}) copy-start(f32[48]{0:T(128)} %copy-done.66) | copy-start | bytes 580
  1070.0 62.4 %copy-start.70 = (f32[48]{0:T(128)S(1)}, f32[48]{0:T(128)}, u32[]{:S(2)}) copy-start(f32[48]{0:T(128)} %copy-done.69) | copy-start | bytes 580
  1070.1 62.4 %copy-start.84 = (f32[48]{0:T(128)S(1)}, f32[48]{0:T(128)}, u32[]{:S(2)}) copy-start(f32[48]{0:T(128)} %param.34) | copy-start | bytes 580
  1070.1 62.4 %copy-start.96 = (f32[48]{0:T(128)S(1)}, f32[48]{0:T(128)}, u32[]{:S(2)}) copy-start(f32[48]{0:T(128)} %param.35) | copy-start | bytes 580
  1071.3 144.8 %copy-start.48 = (bf16[9,32,256]{2,1,0:T(8,128)(2,1)S(1)}, bf16[9,32,256]{2,1,0:T(8,128)(2,1)}, u32[]{:S(2)}) copy-start(bf16[9,32,256]{2,1,0:T(8,128)(2,1)} %param.27) | copy-start | bytes 442372
  1260.5 21.0 %copy-start.92 = (f32[128]{0:T(128)S(1)}, f32[128]{0:T(128)}, u32[]{:S(2)}) copy-start(f32[128]{0:T(128)} %copy-done.91) | copy-start | bytes 1540
  1285.5 13.5 copy-start.98
  1329.8 22.0 %copy-start.76 = (f32[32,4]{0,1:T(4,128)S(1)}, f32[32,4]{0,1:T(4,128)}, u32[]{:S(2)}) copy-start(f32[32,4]{0,1:T(4,128)} %get-tuple-element.142) | copy-start | bytes 1540
  1351.8 99.8 %copy-start.118 = (f32[32]{0:T(128)}, f32[32]{0:T(128)S(1)}, u32[]{:S(2)}) copy-start(f32[32]{0:T(128)S(1)} %get-tuple-element.90) | copy-start | bytes 388
  1351.8 99.8 %copy-start.120 = (f32[32]{0:T(128)}, f32[32]{0:T(128)S(1)}, u32[]{:S(2)}) copy-start(f32[32]{0:T(128)S(1)} %get-tuple-element.91) | copy-start | bytes 388
  1358.5 242.9 %reduce-scatter.17.cloned.1.call-start = ((), (), s32[]{:S(2)}) async-start(), calls=%async_computation.9 | async-start | bytes 1769472 | tf_op jit(solution)/shard_map/reduce_scatter | solution.py:96
  1361.4 410.1 %all-reduce.84.cloned.1.call-start = ((), (), s32[]{:S(2)}) async-start(), calls=%async_computation.17 | async-start | bytes 16711680 | tf_op jit(solution)/shard_map/psum | solution.py:302
  1373.9 24.4 %slice-start.2 = ((s8[8388608]{0:T(1024)(128)(4,1)}), s8[4194304]{0:T(1024)(128)(4,1)S(1)}, s32[]{:S(2)}) async-start(s8[8388608]{0:T(1024)(128)(4,1)} %bitcast.1887), calls=%async_computation.20 | async-start | bytes 8388608
  1386.1 12.3 slice-start.3
  1441.4 8.9 copy-start.13
  1441.4 8.9 copy-start.51
  1450.4 16.7 copy-start.93
  1450.4 17.5 copy-start.39
  1467.8 12.2 copy-start.37
  1480.0 12.4 copy-start.35
  1480.0 25.1 %slice-start = ((s8[8388608]{0:T(1024)(128)(4,1)}), s8[4194304]{0:T(1024)(128)(4,1)S(1)}, s32[]{:S(2)}) async-start(s8[8388608]{0:T(1024)(128)(4,1)} %bitcast.1885), calls=%async_computation.18 | async-start | bytes 8388608
  1492.5 12.7 slice-start.1
  1492.5 12.7 copy-start.33
  1531.6 9.1 copy-start.27
  1540.7 9.1 copy-start.25
  1773.3 8.9 copy-start.57
  (99 other events, 331.3 us)
Sparse Core Ops, SparseCore 0:
  11.0 32.8 reduce-scatter.20
  46.3 48.1 reduce-scatter.18
  97.6 75.0 all-reduce.79
  175.5 32.1 reduce-scatter.22
  359.6 164.5 reduce-scatter.12
  686.1 164.7 reduce-scatter.14
  885.0 79.5 all-gather.3
  1058.8 73.6 all-reduce.81
  1134.2 81.8 all-gather.5
  1358.6 81.2 all-gather.7
  1442.4 32.8 reduce-scatter.16
  1600.8 170.6 all-reduce.83
where the time goes:
time: 1800 us; the launch traced here: 1790 us
  waiting for transfers between devices  820 us (46%)
  matrix products  666 us (37%)
  blocking collectives  122 us (7%)
  local copies, waits for them, and re-layouts  110 us (6%)
  other arithmetic  52 us (3%)
    reduce_scatter x2, waiting for transfers between devices, reduce_channels(): lax.psum_scatter(build_rows(jnp.int32(0), own_rows * lax.axis_size('chan'...  306 us
    dot_general x51, matrix products, conv_rows(): jnp.einsum('cbhw,co->obhw', shifted(inputs, step_down, across), weight[po...  269 us
    dot_general x54, matrix products, conv_back_weight(): jnp.einsum('cbhw,obhw->co', shifted(inputs, step_down, across), gradient,...  200 us
    dot_general x54, matrix products, conv_back_input(): jnp.einsum('obhw,co->cbhw', gradient, weight[position], preferred_element...  158 us
    all_gather x2, waiting for transfers between devices, gather_grads(): return lax.all_gather(values, 'chan', axis=0, tiled=True)  156 us
    psum x1, waiting for transfers between devices, per_device(): lax.psum((point_wgrad, atrous_wgrad, pool_wgrad, proj_wgrad, low_wgrad, d...  148 us
    psum x2, waiting for transfers between devices, channel_total(): return lax.psum(values, 'chan')  120 us
    unnamed x15, waiting for transfers between devices  90.1 us
  transfers between devices with their start and end apart: 12, of which 10 were waited for; matrix products, arithmetic and copies ran while one was open for 18% of the time, Pallas kernels for 0%

commit v1 on v0

v1 whole, which is shorter than its diff:
```python
import functools

import jax
import jax.numpy as jnp
from jax import lax
from jax.experimental import pallas as pl
from jax.experimental.pallas import tpu as pltpu
from jax.sharding import PartitionSpec as P

FA = 32
SCENE_H = 1024
SCENE_W = 2048

epsilon = 1e-05
highest = lax.Precision.HIGHEST
atrous_rates = (6, 12, 18)
f32 = jnp.float32
bf16 = jnp.bfloat16
BOTH = ("crop", "chan")


MESH = pl.DeviceIdType.MESH


def chip_peers(crops, n):
    my_crop, me = lax.axis_index("crop"), lax.axis_index("chan")
    core = lax.rem(me, 2)
    chips = n // 2
    other = (my_crop, me + 1 - 2 * core)
    far = []
    for i in range(crops):
        for j in range(chips):
            if i or j:
                far.append((lax.rem(my_crop + i, crops), lax.rem(me + 2 * j, n)))
    return other, far


def sum_kernel(crops, n, x_ref, o_ref, pair, slots, pair_sems, send, recv):
    other, far = chip_peers(crops, n)
    my_crop, me = lax.axis_index("crop"), lax.axis_index("chan")
    core = lax.rem(me, 2)
    mine = my_crop * (n // 2) + lax.div(me, 2)
    barrier = pltpu.get_barrier_semaphore()
    for peer in [other] + far:
        pl.semaphore_signal(barrier, inc=1, device_id=peer, device_id_type=MESH)
    pl.semaphore_wait(barrier, 1 + len(far))
    pair[core] = x_ref[...]
    copy = pltpu.make_async_remote_copy(
        src_ref=pair.at[core],
        dst_ref=pair.at[core],
        send_sem=pair_sems.at[0],
        recv_sem=pair_sems.at[1],
        device_id=other,
        device_id_type=MESH,
    )
    copy.start()
    copy.wait()
    slots[mine] = pair[0] + pair[1]
    copies = []
    for k, peer in enumerate(far):
        copy = pltpu.make_async_remote_copy(
            src_ref=slots.at[mine],
            dst_ref=slots.at[mine],
            send_sem=send.at[k],
            recv_sem=recv.at[k],
            device_id=peer,
            device_id_type=MESH,
        )
        copy.start()
        copies.append(copy)
    for copy in copies:
        copy.wait()
    o_ref[...] = jnp.sum(slots[...], axis=0)


def sum_all(values, collective_id):
    crops, n = lax.axis_size("crop"), lax.axis_size("chan")
    chips = crops * n // 2
    flat = jnp.concatenate([v.reshape(-1) for v in values])
    rows = -(-flat.shape[0] // 2048) * 8
    flat = jnp.pad(flat, (0, rows * 256 - flat.shape[0])).reshape(rows, 256)
    total = pl.pallas_call(
        functools.partial(sum_kernel, crops, n),
        out_shape=jax.ShapeDtypeStruct((rows, 256), f32),
        in_specs=[pl.BlockSpec(memory_space=pltpu.VMEM)],
        out_specs=pl.BlockSpec(memory_space=pltpu.VMEM),
        scratch_shapes=[
            pltpu.VMEM((2, rows, 256), f32),
            pltpu.VMEM((chips, rows, 256), f32),
            pltpu.SemaphoreType.DMA((2,)),
            pltpu.SemaphoreType.DMA((chips - 1,)),
            pltpu.SemaphoreType.DMA((chips - 1,)),
        ],
        compiler_params=pltpu.CompilerParams(collective_id=collective_id, has_side_effects=True),
    )(flat).reshape(-1)
    outs, at = [], 0
    for v in values:
        outs.append(total[at : at + v.size].reshape(v.shape))
        at += v.size
    return outs


def conv_forward(values, weight, rate, pad):
    kernel = weight.reshape(3, 3, weight.shape[1], weight.shape[2])
    return lax.conv_general_dilated(
        values[None],
        kernel,
        (1, 1),
        ((pad, pad), (rate, rate)),
        rhs_dilation=(rate, rate),
        dimension_numbers=("NHWC", "HWIO", "NHWC"),
        preferred_element_type=f32,
    )[0]


def conv_back_input(gradient, weight, rate, pad):
    kernel = weight.reshape(3, 3, weight.shape[1], weight.shape[2])[::-1, ::-1]
    return lax.conv_general_dilated(
        gradient[None],
        kernel,
        (1, 1),
        ((pad, pad), (rate, rate)),
        rhs_dilation=(rate, rate),
        dimension_numbers=("NHWC", "HWOI", "NHWC"),
        preferred_element_type=f32,
    )[0]


def conv_back_weight(inputs, gradient, rate, pad):
    out = lax.conv_general_dilated(
        inputs,
        gradient,
        (rate, rate),
        ((pad, pad), (rate, rate)),
        dimension_numbers=("CHWN", "IHWO", "HWNC"),
        preferred_element_type=f32,
    )
    return out.reshape(9, inputs.shape[3], gradient.shape[3])


def neighbours(values_up, values_down):
    n = lax.axis_size("chan")
    from_below = lax.ppermute(values_up, "chan", [(i + 1, i) for i in range(n - 1)])
    from_above = lax.ppermute(values_down, "chan", [(i, i + 1) for i in range(n - 1)])
    return from_below, from_above


def with_halo(values):
    from_below, from_above = neighbours(values[:1], values[-1:])
    return jnp.concatenate([from_above, values, from_below], axis=0)


def act_parts(values, average, inverse, scales, shifts):
    normed = (values - average) * inverse
    return normed, scales * normed + shifts


def gelu_back(before, incoming):
    return jax.vjp(jax.nn.gelu, before)[1](incoming)[0]


def moments(totals, samples):
    average = totals[0] / samples
    return average, lax.rsqrt(totals[1] / samples - average * average + epsilon)


def sums_of(values):
    return jnp.stack([jnp.sum(values, axis=(0, 1)), jnp.sum(values * values, axis=(0, 1))])


def grad_sums(pushed, normed):
    return jnp.stack([jnp.sum(pushed * normed, axis=(0, 1)), jnp.sum(pushed, axis=(0, 1))])


def norm_pull(pushed, normed, inverse, scales, totals, samples):
    return (scales * inverse) * (pushed - totals[1] / samples - normed * (totals[0] / samples))


def up_rows(first, count, coarse_first, coarse_count, fine_side):
    fine = first + jnp.arange(count)
    pos = jnp.clip((fine.astype(f32) + 0.5) / 4.0 - 0.5, 0.0, FA - 1.0)
    coarse = (coarse_first + jnp.arange(coarse_count)).astype(f32)
    table = jnp.maximum(0.0, 1.0 - jnp.abs(pos[:, None] - coarse[None, :]))
    return jnp.where(((fine >= 0) & (fine < fine_side))[:, None], table, 0.0)


def own_rows(values, axis):
    size = values.shape[axis] // lax.axis_size("chan")
    return lax.dynamic_slice_in_dim(values, lax.axis_index("chan") * size, size, axis)


def per_device(
    features,
    low_in,
    offsets,
    d_logits,
    w_point,
    w_atrous,
    w_pool,
    w_proj,
    w_low,
    w_dec1,
    w_dec1_low,
    w_dec2,
    w_cls,
    b_cls,
    bn_gain,
    bn_shift,
    low_gain,
    low_shift,
):
    n = lax.axis_size("chan")
    crops = lax.axis_size("crop")
    me = lax.axis_index("chan")
    my_crop = lax.axis_index("crop")
    fine = low_in.shape[2]
    rows = fine // n
    coarse_rows = FA // n
    channels = w_dec2.shape[2]
    c_in = features.shape[1]
    low_width = w_low.shape[1]
    coarse_samples = FA * FA * crops
    fine_samples = fine * fine * crops

    own = w_dec2.shape[1]
    classes = w_cls.shape[1]
    side = w_dec1_low.transpose(2, 0, 1).reshape(own, 9 * low_width)
    tail = jnp.concatenate([side, w_cls], axis=1)
    tail = jnp.pad(tail, ((0, 0), (0, -tail.shape[1] % channels)))
    tail_rows = tail.shape[1] // channels
    tail = tail.reshape(own, tail_rows, channels).transpose(1, 0, 2)
    packed = lax.all_gather(jnp.concatenate([w_proj, w_dec1, tail, w_dec2]), "chan")
    packed = packed.transpose(1, 0, 2, 3).reshape(-1, channels, channels)
    proj_full, dec1_full = packed[:5], packed[5:14]
    tail_full = packed[14 : 14 + tail_rows].transpose(1, 0, 2).reshape(channels, -1)
    dec2_full = packed[14 + tail_rows :]
    dec1_low_full = tail_full[:, : 9 * low_width].reshape(channels, 9, low_width)
    dec1_low_full = dec1_low_full.transpose(1, 2, 0)
    cls_full = tail_full[:, 9 * low_width : 9 * low_width + classes]
    norms = lax.all_gather(jnp.concatenate([bn_gain, bn_shift]), "chan", axis=1, tiled=True)
    gains, shifts = norms[:8], norms[8:]

    row_index = me * rows + jnp.arange(rows, dtype=jnp.int32)
    col_index = jnp.arange(fine, dtype=jnp.int32)
    rows_valid = offsets[0, 0] + 4 * row_index < SCENE_H
    cols_valid = offsets[0, 1] + 4 * col_index < SCENE_W
    mask = (rows_valid[:, None] & cols_valid[None, :]).astype(f32)

    source = features[0].T.reshape(FA, FA, c_in)
    parts = [jnp.einsum("hwc,co->hwo", source, w_point, preferred_element_type=f32)]
    for k in range(3):
        parts.append(conv_forward(source, w_atrous[k], atrous_rates[k], atrous_rates[k]))
    parts = jnp.concatenate([p.astype(bf16) for p in parts], axis=-1)
    low_terms = jnp.einsum("chw,co->how", low_in[0], w_low, preferred_element_type=f32).astype(bf16)
    low_pre = lax.psum_scatter(low_terms, "chan", scatter_dimension=0, tiled=True).astype(f32)
    low_pre = low_pre.transpose(0, 2, 1)
    branch_pre = lax.psum_scatter(parts, "chan", scatter_dimension=0, tiled=True).astype(f32)

    pooled = jnp.mean(features[0].astype(f32), axis=1).astype(bf16)
    pooled_all = lax.all_gather(pooled, "crop", axis=0)
    pool_part = jnp.einsum("bc,co->bo", pooled_all, w_pool, preferred_element_type=f32)
    low_sums, branch_sums, pool_sums = (sums_of(low_pre), sums_of(branch_pre), pool_part)
    low_sums, branch_sums, pool_pre = sum_all([low_sums, branch_sums, pool_sums / crops], 0)

    branch_average, branch_inverse = moments(branch_sums, coarse_samples)
    branch_gain = gains[0:4].reshape(-1)
    branch_normed, branch_before = act_parts(
        branch_pre, branch_average, branch_inverse, branch_gain, shifts[0:4].reshape(-1)
    )
    branch_bf = jax.nn.gelu(branch_before).astype(bf16)

    pool_average = jnp.mean(pool_pre, axis=0)
    pool_inverse = lax.rsqrt(jnp.mean(jnp.square(pool_pre - pool_average), axis=0) + epsilon)
    pool_normed, pool_before = act_parts(pool_pre, pool_average, pool_inverse, gains[4], shifts[4])
    pool_bf = jax.nn.gelu(pool_before).astype(bf16)
    own_pool = lax.dynamic_slice_in_dim(pool_bf, my_crop, 1, 0)

    proj_flat = proj_full[0:4].reshape(4 * channels, channels)
    projected = jnp.einsum("hwc,co->hwo", branch_bf, proj_flat, preferred_element_type=f32)
    projected = projected + jnp.dot(own_pool, proj_full[4], preferred_element_type=f32)
    (merged_sums,) = sum_all([sums_of(projected)], 1)
    merged_average, merged_inverse = moments(merged_sums, coarse_samples)
    merged_normed, merged_before = act_parts(
        projected, merged_average, merged_inverse, gains[5], shifts[5]
    )
    merged = with_halo(jax.nn.gelu(merged_before))

    row_table = up_rows(me * rows - 1, rows + 2, me * coarse_rows - 1, coarse_rows + 2, fine)
    col_table = up_rows(0, fine, 0, FA, fine)
    wide = jnp.einsum("hwc,jw->hjc", merged, col_table, precision=highest)
    upsampled = jnp.einsum("hjc,ih->ijc", wide, row_table, precision=highest).astype(bf16)

    low_average, low_inverse = moments(low_sums, fine_samples)
    low_normed, low_before = act_parts(low_pre, low_average, low_inverse, low_gain, low_shift)
    low_bf = with_halo(jax.nn.gelu(low_before).astype(bf16))

    both_in = jnp.concatenate([upsampled, low_bf], axis=-1)
    dec1_both = jnp.concatenate([dec1_full, dec1_low_full], axis=1)
    dec1_pre = conv_forward(both_in, dec1_both, 1, 0)
    first_average, first_inverse = moments(sum_all([sums_of(dec1_pre)], 2)[0], fine_samples)
    first_normed, first_before = act_parts(
        dec1_pre, first_average, first_inverse, gains[6], shifts[6]
    )
    first_bf = with_halo(jax.nn.gelu(first_before).astype(bf16))

    dec2_pre = conv_forward(first_bf, dec2_full, 1, 0)
    second_average, second_inverse = moments(sum_all([sums_of(dec2_pre)], 3)[0], fine_samples)
    second_normed, second_before = act_parts(
        dec2_pre, second_average, second_inverse, gains[7], shifts[7]
    )
    second_bf = jax.nn.gelu(second_before).astype(bf16)
    logits = jnp.einsum("hwc,co->ohw", second_bf, cls_full, preferred_element_type=f32)
    logits = (logits + b_cls[:, None, None]) * mask

    my_logits = lax.dynamic_slice_in_dim(d_logits[0], me * rows, rows, 1)
    masked = my_logits * mask.astype(bf16)
    cls_bias_grad = jnp.sum(masked.astype(f32), axis=(1, 2))
    cls_weight_grad = jnp.einsum("hwc,ohw->co", second_bf, masked, preferred_element_type=f32)
    second_grad = jnp.einsum("ohw,co->hwc", masked, cls_full, preferred_element_type=f32)
    second_pushed = gelu_back(second_before, second_grad)
    (second_totals,) = sum_all([grad_sums(second_pushed, second_normed)], 4)
    dec2_bf = norm_pull(
        second_pushed, second_normed, second_inverse, gains[7], second_totals, fine_samples
    ).astype(bf16)
    dec2_halo = with_halo(dec2_bf)

    first_grad = conv_back_input(dec2_halo, dec2_full, 1, 0)
    first_pushed = gelu_back(first_before, first_grad)
    (first_totals,) = sum_all([grad_sums(first_pushed, first_normed)], 5)
    dec2_wgrad = conv_back_weight(first_bf[None], dec2_bf[None], 1, 0)
    dec1_bf = norm_pull(
        first_pushed, first_normed, first_inverse, gains[6], first_totals, fine_samples
    ).astype(bf16)
    dec1_halo = with_halo(dec1_bf)

    both_grad = conv_back_input(dec1_halo, dec1_both, 1, 0)
    up_grad, low_act_grad = both_grad[..., :channels], both_grad[..., channels:]
    dec1_wgrad_both = conv_back_weight(both_in[None], dec1_bf[None], 1, 0)

    narrow = jnp.einsum("ijc,jw->iwc", up_grad, col_table, precision=highest)
    merged_part = jnp.einsum("iwc,ih->hwc", narrow, row_table[1:-1], precision=highest)
    from_below, from_above = neighbours(merged_part[:1], merged_part[-1:])
    merged_grad = merged_part[1:-1]
    merged_grad = merged_grad.at[:1].add(from_above).at[-1:].add(from_below)
    merged_pushed = gelu_back(merged_before, merged_grad)
    low_pushed = gelu_back(low_before, low_act_grad)
    merged_totals, low_totals = sum_all(
        [grad_sums(merged_pushed, merged_normed), grad_sums(low_pushed, low_normed)], 6
    )
    proj_bf = norm_pull(
        merged_pushed, merged_normed, merged_inverse, gains[5], merged_totals, coarse_samples
    ).astype(bf16)
    low_pre_bf = norm_pull(
        low_pushed, low_normed, low_inverse, low_gain, low_totals, fine_samples
    ).astype(bf16)

    branch_act_grad = jnp.einsum("hwo,co->hwc", proj_bf, proj_flat, preferred_element_type=f32)
    proj_wgrad_flat = jnp.einsum("hwc,hwo->co", branch_bf, proj_bf, preferred_element_type=f32)
    branch_pushed = gelu_back(branch_before, branch_act_grad)
    crop_slot = (jnp.arange(crops) == my_crop).astype(f32)
    proj_sums = crop_slot[:, None] * jnp.sum(proj_bf.astype(f32), axis=(0, 1))[None]
    branch_totals, proj_sums, cls_weight_grad, cls_bias_grad = sum_all(
        [grad_sums(branch_pushed, branch_normed), proj_sums, cls_weight_grad, cls_bias_grad], 7
    )
    branch_grad = norm_pull(
        branch_pushed, branch_normed, branch_inverse, branch_gain, branch_totals, coarse_samples
    ).astype(bf16)
    branch_full = lax.all_gather(branch_grad, "chan", axis=0, tiled=True)
    branch_all = lax.all_gather(branch_full, "crop", axis=0)
    source_all = lax.all_gather(source, "crop", axis=0)

    pool_act_grad = jnp.einsum("co,bo->bc", proj_full[4].astype(f32), proj_sums, precision=highest)
    proj_wgrad_pool = jnp.einsum("bc,bo->co", pool_bf.astype(f32), proj_sums, precision=highest)
    pool_pushed = gelu_back(pool_before, pool_act_grad)
    pool_totals = jnp.stack([jnp.sum(pool_pushed * pool_normed, 0), jnp.sum(pool_pushed, 0)])
    pool_grad = norm_pull(
        pool_pushed, pool_normed, pool_inverse, gains[4], pool_totals, crops
    ).astype(bf16)
    own_pool_grad = lax.dynamic_slice_in_dim(pool_grad, my_crop, 1, 0)
    pool_wgrad = jnp.einsum("bc,bo->co", pooled_all, pool_grad, preferred_element_type=f32)

    low_full = lax.all_gather(low_pre_bf.transpose(0, 2, 1), "chan", axis=0, tiled=True)
    low_wgrad = jnp.einsum("chw,how->co", low_in[0], low_full, preferred_element_type=f32)
    early_grad = jnp.einsum("how,co->chw", low_full, w_low, preferred_element_type=f32)

    by_branch = lambda v, k: v[..., k * channels : (k + 1) * channels]
    source_grad = jnp.einsum(
        "hwo,co->hwc", by_branch(branch_full, 0), w_point, preferred_element_type=f32
    )
    point_wgrad = jnp.einsum(
        "bhwc,bhwo->co", source_all, by_branch(branch_all, 0), preferred_element_type=f32
    )
    atrous_wgrad = []
    for k in range(3):
        rate = atrous_rates[k]
        source_grad = source_grad + conv_back_input(
            by_branch(branch_full, k + 1), w_atrous[k], rate, rate
        )
        atrous_wgrad.append(
            conv_back_weight(source_all, by_branch(branch_all, k + 1), rate, rate)
        )
    pooled_grad = jnp.einsum("bo,co->bc", own_pool_grad, w_pool, preferred_element_type=f32)
    source_grad = source_grad + pooled_grad[0] / (FA * FA)

    scatter = lambda v, axis: lax.psum_scatter(v, "chan", scatter_dimension=axis, tiled=True)
    side_part = dec1_wgrad_both[:, channels:].transpose(2, 0, 1).reshape(channels, -1)
    side_size = side_part.shape[1]
    side_part = jnp.pad(side_part, ((0, 0), (0, -side_size % channels)))
    side_part = side_part.reshape(channels, -1, channels).transpose(1, 0, 2)
    blocks = jnp.concatenate(
        [
            dec2_wgrad.astype(bf16),
            dec1_wgrad_both[:, :channels].astype(bf16),
            proj_wgrad_flat.reshape(4, channels, channels).astype(bf16),
            side_part.astype(bf16),
        ]
    )
    blocks = blocks.reshape(-1, n, own, channels).transpose(1, 0, 2, 3)
    blocks = lax.psum_scatter(blocks, "chan", scatter_dimension=0, tiled=False).astype(f32)
    blocks, low_wgrad = lax.psum((blocks, low_wgrad), "crop")
    dec2_wgrad, dec1_wgrad, proj_wgrad = blocks[:9], blocks[9:18], blocks[18:22]
    side_wgrad = blocks[22:].transpose(1, 0, 2).reshape(own, -1)[:, :side_size]
    side_wgrad = side_wgrad.reshape(own, 9, low_width).transpose(1, 2, 0)
    proj_wgrad = jnp.concatenate([proj_wgrad, own_rows(proj_wgrad_pool, 0)[None]], axis=0)

    gain_rows = [branch_totals[0].reshape(4, -1), pool_totals[0:1], merged_totals[0:1]]
    gain_rows += [first_totals[0:1], second_totals[0:1]]
    shift_rows = [branch_totals[1].reshape(4, -1), pool_totals[1:2], merged_totals[1:2]]
    shift_rows += [first_totals[1:2], second_totals[1:2]]
    return (
        logits[None],
        source_grad.reshape(FA * FA, c_in).T[None],
        early_grad[None],
        point_wgrad,
        jnp.stack(atrous_wgrad),
        pool_wgrad,
        proj_wgrad,
        low_wgrad,
        dec1_wgrad,
        side_wgrad,
        dec2_wgrad,
        own_rows(cls_weight_grad, 0),
        cls_bias_grad,
        own_rows(jnp.concatenate(gain_rows), 1),
        own_rows(jnp.concatenate(shift_rows), 1),
        low_totals[0],
        low_totals[1],
    )


def solution(mesh):
    placed = (
        P("crop", "chan", None),
        P("crop", "chan", None, None),
        P("crop", None),
        P("crop", None, None, None),
        P("chan", None),
        P(None, None, "chan", None),
        P("chan", None),
        P(None, "chan", None),
        P("chan", None),
        P(None, "chan", None),
        P(None, None, "chan"),
        P(None, "chan", None),
        P("chan", None),
        P(),
        P(None, "chan"),
        P(None, "chan"),
        P(),
        P(),
    )
    return jax.shard_map(
        per_device,
        mesh=mesh,
        in_specs=placed,
        out_specs=(
            P("crop", None, "chan", None),
            P("crop", "chan", None),
            P("crop", "chan", None, None),
            P("chan", None),
            P(None, None, "chan", None),
            P("chan", None),
            P(None, "chan", None),
            P("chan", None),
            P(None, "chan", None),
            P(None, None, "chan"),
            P(None, "chan", None),
            P("chan", None),
            P(),
            P(None, "chan"),
            P(None, "chan"),
            P(),
            P(),
        ),
        check_vma=False,
    )
```

time: 1800 us -> 817 us (0.45)
  waiting for transfers between devices: 820 us -> 243 us
  matrix products: 666 us -> 243 us
  Pallas kernels: 0 us -> 118 us
  blocking collectives: 122 us -> 40.6 us
  local copies, waits for them, and re-layouts: 110 us -> 65.7 us
  starting transfers between devices: 1.94 us -> 21.9 us
    dot_general x177 -> x22, matrix products: 663 us -> 31.2 us  [the longest x1 3.35 us: per_device(): jnp.einsum('ohw,co->hwc', masked, cls_full, preferred_element_type=f32)]
    reduce_scatter x3 -> x2, waiting for transfers between devices: 306 us -> 7.34 us  [the longest x1 7.34 us: per_device(): lax.psum_scatter(parts, 'chan', scatter_dimension=0, tiled=True).astype(f32)]
    psum x3 -> x1, waiting for transfers between devices: 268 us -> 43.5 us  [per_device(): blocks, low_wgrad = lax.psum((blocks, low_wgrad), 'crop')]
    conv_general_dilated x0 -> x15, matrix products: none -> 212 us  [the longest x5 91.8 us: conv_back_weight(): lax.conv_general_dilated(inputs, gradient, (rate, rate), ((pad, pad), (ra...]
    pallas_call x0 -> x8, Pallas kernels: none -> 118 us  [sum_all(): pl.pallas_call(functools.partial(sum_kernel, crops, n), out_shape=jax.Sha...]
    psum x8 -> x1, blocking collectives: 87 us -> 16.8 us  [per_device(): blocks, low_wgrad = lax.psum((blocks, low_wgrad), 'crop')]
    unnamed x15 -> x10, waiting for transfers between devices: 90.1 us -> 51.6 us
    add x3 -> x0, local copies, waits for them, and re-layouts: 36.6 us -> none  [the longest x2 36.1 us: conv_rows(): result = tap_term if result is None else result + tap_term]
  transfers between devices with their start and end apart: 12 -> 21, of which waited for: 10 -> 11; matrix products, arithmetic and copies ran while one was open for 18% -> 20% of each run, Pallas kernels for 0% -> 5%
where the time goes in v1:
time: 817 us; the launch traced here: 805 us
  matrix products  243 us (30%)
  waiting for transfers between devices  243 us (30%)
  Pallas kernels  118 us (14%)
  local copies, waits for them, and re-layouts  65.7 us (8%)
  other arithmetic  57 us (7%)
  blocking collectives  40.6 us (5%)
  starting transfers between devices  21.9 us (3%)
  between operations  16.3 us (2%)
    pallas_call x8, Pallas kernels, sum_all(): pl.pallas_call(functools.partial(sum_kernel, crops, n), out_shape=jax.Sha...  118 us
    conv_general_dilated x5, matrix products, conv_back_weight(): lax.conv_general_dilated(inputs, gradient, (rate, rate), ((pad, pad), (ra...  91.8 us
    conv_general_dilated x5, matrix products, conv_forward(): lax.conv_general_dilated(values[None], kernel, (1, 1), ((pad, pad), (rate...  60.7 us
    conv_general_dilated x5, matrix products, conv_back_input(): lax.conv_general_dilated(gradient[None], kernel, (1, 1), ((pad, pad), (ra...  59.8 us
    unnamed x10, waiting for transfers between devices  51.6 us
    psum x1, waiting for transfers between devices, per_device(): blocks, low_wgrad = lax.psum((blocks, low_wgrad), 'crop')  43.5 us
    all_gather x1, waiting for transfers between devices, per_device(): branch_all = lax.all_gather(branch_full, 'crop', axis=0)  39.3 us
    all_gather x1, waiting for transfers between devices, per_device(): source_all = lax.all_gather(source, 'crop', axis=0)  31.1 us
  transfers between devices with their start and end apart: 21, of which 11 were waited for; matrix products, arithmetic and copies ran while one was open for 20% of the time, Pallas kernels for 5%

profile of v1, /device:TPU:0, one launch (start us, length us, event | category | flops | bytes accessed | tf_op | source)
XLA Modules:
  0.0 805.1 jit_solution(17845862347658244518)
XLA Ops:
  8.4 2.7 fusion.75
  11.5 3.9 fusion.255
  15.4 9.9 %fusion.104 = bf16[1,32,32,256]{3,0,2,1:T(2,128)(2,1)S(1)} fusion(bf16[3,3,256,256]{3,2,1,0:T(8,128)(2,1)} %bitcast.419, bf16[1,32,32,256]{3,2,1,0:T(8,128)(2,1)S(1)} %bitcast.401), kind=kOutput, calls=%fused_computation.146 | convolution fusion | flops 471859200 | bytes 2228224 | tf_op jit(solution)/shard_map/conv_general_dilated | solution.py:105
  26.6 7.9 fusion.106
  34.5 6.8 fusion.108
  45.4 15.7 %all-gather.3 = f32[8,32,16]{1,2,0:T(8,128)S(1)} all-gather(f32[1,32,16]{1,2,0:T(8,128)S(1)} %maximum_bitcast_fusion.4), channel_id=1, replica_groups=mesh['crop'=4,'chan'=8] {'chan'}, dimensions={0}, use_global_device_ids=true | all-gather | bytes 18432 | tf_op jit(solution)/shard_map/all_gather | solution.py:240
  61.4 8.1 %all-gather.4 = bf16[4,1,256]{2,1,0:T(2,128)(2,1)S(1)} all-gather(bf16[1,1,256]{2,1,0:T(2,128)(2,1)S(1)} %reshape.694), channel_id=3, replica_groups=mesh['crop'=4,'chan'=8] {'crop'}, dimensions={0}, use_global_device_ids=true | all-gather | bytes 2560 | tf_op jit(solution)/shard_map/all_gather | solution.py:260
  77.4 7.3 reduce-scatter.6.cloned.1.call-done
  86.5 15.7 %shard_map.305 = f32[16,256]{1,0:T(8,128)} custom-call(f32[16,256]{1,0:T(8,128)} %reshape.654.x_ref), custom_call_target="tpu_custom_call" | custom-call | tf_op jit(solution)/shard_map/pallas_call | solution.py:82
  108.8 3.4 collective-permute-done.3
  112.7 15.2 %all-gather.17.cloned.1.call-done = bf16[200,32,256]{2,1,0:T(8,128)(2,1)} async-done(((bf16[25,32,256]{2,1,0:T(8,128)(2,1)}), bf16[200,32,256]{2,1,0:T(8,128)(2,1)}) %all-gather.17.cloned.1.call-update) | async-done | bytes 3276816 | tf_op jit(solution)/shard_map/all_gather | solution.py:232
  127.9 2.3 copy.448
  133.9 10.3 %shard_map.306 = f32[8,256]{1,0:T(8,128)} custom-call(f32[8,256]{1,0:T(8,128)} %reshape.660.x_ref), custom_call_target="tpu_custom_call" | custom-call | tf_op jit(solution)/shard_map/pallas_call | solution.py:82
  148.6 3.4 fusion.256
  154.1 3.1 convolution_convert_fusion
  158.4 19.9 %fusion.269 = (f32[256]{0:T(256)S(1)}, f32[1,16,128,256]{3,0,2,1:T(1,128)S(1)}) fusion(bf16[3,3,48,256]{3,2,1,0:T(8,128)(2,1)S(1)} %bitcast.443, bf16[3,3,256,256]{3,2,1,0:T(8,128)(2,1)S(1)} %bitcast.425, bf16[1,18,128,304]{3,1,2,0:T(8,128)(2,1)S(1)} %maximum_bitcast_fusion), kind=kOutput, calls=%fused_computation.408 | convolution fusion | flops 2857287424 | bytes 4899840 | tf_op jit(solution)/shard_map/conv_general_dilated | solution.py:105
  179.5 13.1 %shard_map.307 = f32[8,256]{1,0:T(8,128)} custom-call(f32[8,256]{1,0:T(8,128)} %reshape.663.x_ref), custom_call_target="tpu_custom_call" | custom-call | tf_op jit(solution)/shard_map/pallas_call | solution.py:82
  200.7 16.1 %fusion.270 = (f32[256]{0:T(256)S(1)}, f32[1,16,128,256]{3,0,2,1:T(1,128)S(1)}) fusion(bf16[3,3,256,256]{3,2,1,0:T(8,128)(2,1)S(1)} %bitcast.428, bf16[1,18,128,256]{3,2,1,0:T(8,128)(2,1)S(1)} %maximum_bitcast_fusion.1), kind=kOutput, calls=%fused_computation.409 | convolution fusion | flops 2403860224 | bytes 4457472 | tf_op jit(solution)/shard_map/conv_general_dilated | solution.py:105
  218.0 13.4 %shard_map.308 = f32[8,256]{1,0:T(8,128)} custom-call(f32[8,256]{1,0:T(8,128)} %reshape.666.x_ref), custom_call_target="tpu_custom_call" | custom-call | tf_op jit(solution)/shard_map/pallas_call | solution.py:82
  232.3 3.4 multiply_reduce_fusion.1
  236.3 11.0 %shard_map.309 = f32[8,256]{1,0:T(8,128)} custom-call(f32[8,256]{1,0:T(8,128)} %reshape.668.x_ref), custom_call_target="tpu_custom_call" | custom-call | tf_op jit(solution)/shard_map/pallas_call | solution.py:82
  248.7 2.2 multiply_convert_fusion.1
  251.5 2.1 collective-permute-start.6
  255.1 14.2 %fusion.70 = bf16[3,3,256,256]{3,2,1,0:T(8,128)(2,1)} fusion(bf16[1,16,128,256]{3,2,1,0:T(8,128)(2,1)S(1)} %bitcast.406, bf16[1,18,128,256]{3,2,1,0:T(8,128)(2,1)S(1)} %copy-done.24), kind=kOutput, calls=%fused_computation.97 | convolution fusion | flops 2403926016 | bytes 3407872 | tf_op jit(solution)/shard_map/conv_general_dilated | solution.py:130
  270.6 15.7 %fusion.4 = f32[1,16,128,256]{3,0,2,1:T(1,128)S(1)} fusion(bf16[3,3,256,256]{3,2,1,0:T(8,128)(2,1)S(1)} %bitcast.429, bf16[1,18,128,256]{3,2,1,0:T(8,128)(2,1)S(1)} %maximum_bitcast_fusion.2), kind=kOutput, calls=%fused_computation.15 | convolution fusion | flops 2403336192 | bytes 4456448 | tf_op jit(solution)/shard_map/conv_general_dilated | solution.py:118
  286.4 2.9 multiply_reduce_fusion
  290.0 13.6 %shard_map.310 = f32[8,256]{1,0:T(8,128)} custom-call(f32[8,256]{1,0:T(8,128)} %reshape.670.x_ref), custom_call_target="tpu_custom_call" | custom-call | tf_op jit(solution)/shard_map/pallas_call | solution.py:82
  305.0 4.3 fusion.29
  311.4 2.2 collective-permute-start.8
  313.6 1.7 collective-permute-start.9
  315.3 19.8 %fusion.65 = bf16[3,3,304,256]{3,2,1,0:T(8,128)(2,1)S(1)} fusion(bf16[1,16,128,256]{3,2,1,0:T(8,128)(2,1)} %fusion.29, bf16[1,18,128,304]{3,1,2,0:T(8,128)(2,1)} %copy-done.16), kind=kOutput, calls=%fused_computation.95 | convolution fusion | flops 2854662144 | bytes 3850240 | tf_op jit(solution)/shard_map/conv_general_dilated | solution.py:130
  338.2 21.4 %fusion.6 = f32[1,16,128,304]{3,0,2,1:T(1,128)} fusion(bf16[1,18,128,256]{3,2,1,0:T(8,128)(2,1)S(1)} %maximum_bitcast_fusion.3, bf16[3,3,48,256]{3,2,1,0:T(8,128)(2,1)S(1)} %bitcast.444, bf16[3,3,256,256]{3,2,1,0:T(8,128)(2,1)S(1)} %bitcast.426), kind=kOutput, calls=%fused_computation.17 | convolution fusion | flops 2856763392 | bytes 5070848 | tf_op jit(solution)/shard_map/conv_general_dilated | solution.py:118
  359.6 7.4 copy.244
  367.1 3.0 fusion.80
  372.1 3.7 collective-permute-start.10
  386.2 13.4 %shard_map.311 = f32[8,256]{1,0:T(8,128)} custom-call(f32[8,256]{1,0:T(8,128)} %reshape.673.x_ref), custom_call_target="tpu_custom_call" | custom-call | tf_op jit(solution)/shard_map/pallas_call | solution.py:82
  404.6 1.9 pad_maximum_fusion.1
  408.1 2.0 convolution_bitcast_fusion.3
  411.8 2.5 fusion.127
  415.0 27.1 %shard_map.312 = f32[40,256]{1,0:T(8,128)} custom-call(f32[40,256]{1,0:T(8,128)} %reshape.676.x_ref), custom_call_target="tpu_custom_call" | custom-call | tf_op jit(solution)/shard_map/pallas_call | solution.py:82
  442.9 2.0 fusion.130
  445.5 50.8 %all-reduce.16.cloned.1.call-done = bf16[8,24,32,256]{3,2,0,1:T(8,128)(2,1)} async-done(((bf16[8,24,32,256]{3,2,0,1:T(8,128)(2,1)}), bf16[8,24,32,256]{3,2,0,1:T(8,128)(2,1)}) %all-reduce.16.cloned.1.call-update) | async-done | bytes 3145744
  496.3 2.6 bitcast_convert_fusion
  499.6 1.9 fusion.159
  501.6 25.7 %all-gather.11.cloned.1.call-done = bf16[32,32,1024]{2,1,0:T(8,128)(2,1)} async-done(((bf16[4,32,1024]{2,1,0:T(8,128)(2,1)}), bf16[32,32,1024]{2,1,0:T(8,128)(2,1)}) %all-gather.11.cloned.1.call-update) | async-done | bytes 2097168 | tf_op jit(solution)/shard_map/all_gather | solution.py:368
  528.3 1.8 fusion.87
  535.5 43.5 %all-reduce.14.cloned.1.call-done = f32[24,32,256]{2,1,0:T(8,128)} async-done(((f32[24,32,256]{2,1,0:T(8,128)}), f32[24,32,256]{2,1,0:T(8,128)}) %all-reduce.14.cloned.1.call-update) | async-done | bytes 786448 | tf_op jit(solution)/shard_map/psum | solution.py:420
  582.3 1.9 fusion.260
  584.2 22.2 %all-gather.13.cloned.1.call-done = bf16[128,48,128]{2,1,0:T(8,128)(2,1)} async-done(((bf16[16,48,128]{2,1,0:T(8,128)(2,1)}), bf16[128,48,128]{2,1,0:T(8,128)(2,1)}) %all-gather.13.cloned.1.call-update) | async-done | bytes 1572880 | tf_op jit(solution)/shard_map/all_gather | solution.py:382
  606.4 1.8 convolution_bitcast_fusion
  608.2 2.5 copy.275
  611.7 16.8 %psum.15 = f32[32,48]{1,0:T(8,128)} all-reduce(f32[32,48]{1,0:T(8,128)S(1)} %convolution_bitcast_fusion.4), channel_id=1, replica_groups=mesh['crop'=4,'chan'=8] {'crop'}, use_global_device_ids=true, to_apply=%region_31.32 | all-reduce | flops 1536 | bytes 12288 | tf_op jit(solution)/shard_map/psum | solution.py:420
  629.8 7.4 fusion.97
  637.2 8.5 %fusion.95 = f32[1,32,32,256]{3,0,2,1:T(1,128)S(1)} fusion(bf16[3,3,256,256]{3,2,1,0:T(8,128)(2,1)S(1)} %bitcast.420, bf16[1,32,32,256]{3,2,1,0:T(8,128)(2,1)S(1)} %get-tuple-element.166), kind=kOutput, calls=%fused_computation.130 | convolution fusion | flops 471859200 | bytes 2752512 | tf_op jit(solution)/shard_map/conv_general_dilated | solution.py:118
  645.7 6.8 fusion.99
  653.9 2.5 copy.257
  656.4 39.3 %all-gather.19.cloned.1.call-done = bf16[128,32,1024]{2,1,0:T(8,128)(2,1)} async-done(((bf16[32,32,1024]{2,1,0:T(8,128)(2,1)}), bf16[128,32,1024]{2,1,0:T(8,128)(2,1)}) %all-gather.19.cloned.1.call-update) | async-done | bytes 8388624 | tf_op jit(solution)/shard_map/all_gather | solution.py:369
  695.7 6.2 fusion.254
  701.9 31.1 %all-gather.15.cloned.1.call-done = bf16[4,32,32,256]{3,2,1,0:T(8,128)(2,1)} async-done(((bf16[1,32,32,256]{3,2,1,0:T(8,128)(2,1)}), bf16[4,32,32,256]{3,2,1,0:T(8,128)(2,1)}) %all-gather.15.cloned.1.call-update) | async-done | bytes 2097168 | tf_op jit(solution)/shard_map/all_gather | solution.py:370
  733.0 3.0 fusion.83
  736.8 21.6 %fusion.54 = f32[3,3,256,256]{3,2,1,0:T(8,128)S(1)} fusion(bf16[4,32,32,256]{3,2,1,0:T(8,128)(2,1)} %get-tuple-element.157, bf16[4,32,32,256]{3,2,1,0:T(8,128)(2,1)} %all-gather.15.cloned.1.call-done), kind=kOutput, calls=%fused_computation.73 | convolution fusion | flops 3699376128 | bytes 6553600 | tf_op jit(solution)/shard_map/conv_general_dilated | solution.py:130
  758.5 13.8 %fusion.50 = f32[3,3,256,256]{3,2,1,0:T(8,128)S(1)} fusion(bf16[4,32,32,256]{3,2,1,0:T(8,128)(2,1)S(1)} %copy-done.17, bf16[4,32,32,256]{3,2,1,0:T(8,128)(2,1)S(1)} %copy-done.128), kind=kOutput, calls=%fused_computation.69 | convolution fusion | flops 1887436800 | bytes 6553600 | tf_op jit(solution)/shard_map/conv_general_dilated | solution.py:130
  772.3 22.4 %fusion.52 = f32[3,3,256,256]{3,2,1,0:T(8,128)S(1)} fusion(bf16[4,32,32,256]{3,2,1,0:T(8,128)(2,1)S(1)} %get-tuple-element.159, bf16[4,32,32,256]{3,2,1,0:T(8,128)(2,1)S(1)} %copy-done.128), kind=kOutput, calls=%fused_computation.71 | convolution fusion | flops 2717908992 | bytes 6553600 | tf_op jit(solution)/shard_map/conv_general_dilated | solution.py:130
  794.7 3.7 pad_maximum_fusion
  (475 shorter events, 95.3 us)
Async XLA Ops:
  7.2 69.0 %reduce-scatter.8.cloned.1.call-start = ((), (), s32[]{:S(2)}) async-start(), calls=%async_computation.3 | async-start | bytes 1769472 | tf_op jit(solution)/shard_map/reduce_scatter | solution.py:255
  11.2 73.5 %reduce-scatter.6.cloned.1.call-start = ((), (), s32[]{:S(2)}) async-start(), calls=%async_computation.2 | async-start | bytes 2359296 | tf_op jit(solution)/shard_map/reduce_scatter | solution.py:257
  11.5 49.8 %copy-start.9 = (bf16[1,256,1024]{1,2,0:T(8,128)(2,1)}, bf16[1,256,1024]{1,2,0:T(8,128)(2,1)S(1)}, u32[]{:S(2)}) copy-start(bf16[1,256,1024]{1,2,0:T(8,128)(2,1)S(1)} %copy.229) | copy-start | bytes 1572868
  15.4 19.1 %copy-start.18 = (bf16[1,9,256,256]{3,2,1,0:T(8,128)(2,1)}, bf16[1,9,256,256]{3,2,1,0:T(8,128)(2,1)S(1)}, u32[]{:S(2)}) copy-start(bf16[1,9,256,256]{3,2,1,0:T(8,128)(2,1)S(1)} %get-tuple-element.160) | copy-start | bytes 3538948
  43.3 26.2 %copy-start.39 = (bf16[256,256]{1,0:T(8,128)(2,1)S(1)}, bf16[256,256]{1,0:T(8,128)(2,1)}, u32[]{:S(2)}) copy-start(bf16[256,256]{1,0:T(8,128)(2,1)} %param.28) | copy-start | bytes 393220
  43.3 26.4 %copy-start.121 = (s32[1,2]{1,0:T(1,128)S(1)}, s32[1,2]{1,0:T(1,128)}, u32[]{:S(2)}) copy-start(s32[1,2]{1,0:T(1,128)} %param.24) | copy-start | bytes 28
  43.4 60.3 %copy-start.102 = (f32[48]{0:T(128)S(1)}, f32[48]{0:T(128)}, u32[]{:S(2)}) copy-start(f32[48]{0:T(128)} %param.38) | copy-start | bytes 580
  43.4 60.9 %copy-start.118 = (f32[48]{0:T(128)S(1)}, f32[48]{0:T(128)}, u32[]{:S(2)}) copy-start(f32[48]{0:T(128)} %param.39) | copy-start | bytes 580
  43.4 84.6 %all-gather.17.cloned.1.call-start = ((), (), s32[]{:S(2)}) async-start(), calls=%async_computation.8 | async-start | bytes 3686400 | tf_op jit(solution)/shard_map/all_gather | solution.py:232
  45.3 451.0 %all-reduce.16.cloned.1.call-start = ((), (), s32[]{:S(2)}) async-start(), calls=%async_computation.10 | async-start | bytes 6291456
  61.2 71.6 %copy-start.82 = (f32[1,2,4,128]{3,1,2,0:T(2,128)}, f32[1,2,4,128]{3,1,2,0:T(2,128)S(1)}, u32[]{:S(2)}) copy-start(f32[1,2,4,128]{3,1,2,0:T(2,128)S(1)} %copy.297) | copy-start | bytes 12292
  61.2 71.6 %copy-start.108 = (f32[1,2,4,128]{3,1,2,0:T(2,128)}, f32[1,2,4,128]{3,1,2,0:T(2,128)S(1)}, u32[]{:S(2)}) copy-start(f32[1,2,4,128]{3,1,2,0:T(2,128)S(1)} %copy.301) | copy-start | bytes 12292
  69.7 83.5 %copy-start.123 = (pred[128]{0:T(512)(128)(4,1)}, pred[128]{0:T(512)(128)(4,1)S(1)}, u32[]{:S(2)}) copy-start(pred[128]{0:T(512)(128)(4,1)S(1)} %iota_compare_fusion.3) | copy-start | bytes 388
  69.7 83.5 %copy-start.124 = (f32[128]{0:T(128)}, f32[128]{0:T(128)S(1)}, u32[]{:S(2)}) copy-start(f32[128]{0:T(128)S(1)} %add_clamp_fusion) | copy-start | bytes 1540
  69.7 83.5 %copy-start.125 = (f32[32]{0:T(128)}, f32[32]{0:T(128)S(1)}, u32[]{:S(2)}) copy-start(f32[32]{0:T(128)S(1)} %iota_convert_fusion) | copy-start | bytes 388
  103.6 29.2 %copy-start.78 = (f32[1024]{0:T(1024)}, f32[1024]{0:T(1024)S(1)}, u32[]{:S(2)}) copy-start(f32[1024]{0:T(1024)S(1)} %get-tuple-element.198) | copy-start | bytes 12292
  103.6 29.2 %copy-start.80 = (f32[1024]{0:T(1024)}, f32[1024]{0:T(1024)S(1)}, u32[]{:S(2)}) copy-start(f32[1024]{0:T(1024)S(1)} %get-tuple-element.199) | copy-start | bytes 12292
  105.5 3.3 collective-permute-start.2
  106.8 5.5 collective-permute-start.3
  108.1 22.2 %copy-start.66 = (f32[256]{0:T(256)}, f32[256]{0:T(256)S(1)}, u32[]{:S(2)}) copy-start(f32[256]{0:T(256)S(1)} %broadcast_multiply_fusion.8) | copy-start | bytes 3076
  108.1 22.2 %copy-start.64 = (f32[256]{0:T(256)}, f32[256]{0:T(256)S(1)}, u32[]{:S(2)}) copy-start(f32[256]{0:T(256)S(1)} %add_rsqrt_fusion.3) | copy-start | bytes 3076
  108.7 36.8 %copy-start.72 = (f32[1,256]{1,0:T(1,128)}, f32[1,256]{1,0:T(1,128)S(1)}, u32[]{:S(2)}) copy-start(f32[1,256]{1,0:T(1,128)S(1)} %get-tuple-element.193) | copy-start | bytes 3076
  108.7 36.9 %copy-start.86 = (f32[1,256]{1,0:T(1,128)}, f32[1,256]{1,0:T(1,128)S(1)}, u32[]{:S(2)}) copy-start(f32[1,256]{1,0:T(1,128)S(1)} %get-tuple-element.190) | copy-start | bytes 3076
  108.7 85.2 %copy-start.60 = (f32[1,256]{1,0:T(1,128)}, f32[1,256]{1,0:T(1,128)S(1)}, u32[]{:S(2)}) copy-start(f32[1,256]{1,0:T(1,128)S(1)} %get-tuple-element.194) | copy-start | bytes 3076
  108.7 85.2 %copy-start.70 = (f32[1,256]{1,0:T(1,128)}, f32[1,256]{1,0:T(1,128)S(1)}, u32[]{:S(2)}) copy-start(f32[1,256]{1,0:T(1,128)S(1)} %get-tuple-element.189) | copy-start | bytes 3076
  108.8 123.5 %copy-start.106 = (f32[1,256]{1,0:T(1,128)}, f32[1,256]{1,0:T(1,128)S(1)}, u32[]{:S(2)}) copy-start(f32[1,256]{1,0:T(1,128)S(1)} %get-tuple-element.195) | copy-start | bytes 3076
  108.8 123.5 %copy-start.126 = (f32[1,256]{1,0:T(1,128)}, f32[1,256]{1,0:T(1,128)S(1)}, u32[]{:S(2)}) copy-start(f32[1,256]{1,0:T(1,128)S(1)} %get-tuple-element.188) | copy-start | bytes 3076
  108.8 23.2 %copy-start.84 = (bf16[4,256]{1,0:T(4,128)(2,1)}, bf16[4,256]{1,0:T(4,128)(2,1)S(1)}, u32[]{:S(2)}) copy-start(bf16[4,256]{1,0:T(4,128)(2,1)S(1)} %multiply_convert_fusion.7) | copy-start | bytes 6148
  133.3 18.7 %copy-start.27 = (f32[4,32,256]{2,1,0:T(8,128)}, f32[4,32,256]{2,1,0:T(8,128)S(1)}, u32[]{:S(2)}) copy-start(f32[4,32,256]{2,1,0:T(8,128)S(1)} %get-tuple-element.233) | copy-start | bytes 393220
  145.7 7.5 collective-permute-start
  147.3 5.9 collective-permute-start.1
  153.1 79.2 %copy-start.36 = (bf16[2,256,256]{1,2,0:T(8,128)(2,1)}, bf16[2,256,256]{1,2,0:T(8,128)(2,1)S(1)}, u32[]{:S(2)}) copy-start(bf16[2,256,256]{1,2,0:T(8,128)(2,1)S(1)} %copy.227) | copy-start | bytes 786436
  157.6 20.8 %copy-start.16 = (bf16[1,18,128,304]{3,1,2,0:T(8,128)(2,1)}, bf16[1,18,128,304]{3,1,2,0:T(8,128)(2,1)S(1)}, u32[]{:S(2)}) copy-start(bf16[1,18,128,304]{3,1,2,0:T(8,128)(2,1)S(1)} %maximum_bitcast_fusion) | copy-start | bytes 4202500
  194.9 3.9 collective-permute-start.4
  196.6 3.8 collective-permute-start.5
  216.8 31.8 %copy-start.6 = (f32[1,16,128,256]{3,0,2,1:T(1,128)}, f32[1,16,128,256]{3,0,2,1:T(1,128)S(1)}, u32[]{:S(2)}) copy-start(f32[1,16,128,256]{3,0,2,1:T(1,128)S(1)} %get-tuple-element.237) | copy-start | bytes 6291460
  251.5 17.8 %collective-permute-start.6 = (bf16[1,128,256]{2,1,0:T(8,128)(2,1)}, bf16[1,128,256]{2,1,0:T(8,128)(2,1)}, u32[]{:S(2)}, u32[]{:S(2)}) collective-permute-start(bf16[1,128,256]{2,1,0:T(8,128)(2,1)} %get-tuple-element.170), channel_id=1, source_target_pairs={{0,1},{1,2},{2,3},{3,4},{4,5},{5,6},{6,7},{8,9},{9,10},{10,11},{11... | collective-permute-start | bytes 196616 | tf_op jit(solution)/shard_map/ppermute | solution.py:144
  253.6 15.6 %collective-permute-start.7 = (bf16[1,128,256]{2,1,0:T(8,128)(2,1)}, bf16[1,128,256]{2,1,0:T(8,128)(2,1)}, u32[]{:S(2)}, u32[]{:S(2)}) collective-permute-start(bf16[1,128,256]{2,1,0:T(8,128)(2,1)} %get-tuple-element.171), channel_id=1, source_target_pairs={{1,0},{2,1},{3,2},{4,3},{5,4},{6,5},{7,6},{9,8},{10,9},{11,10},{12... | collective-permute-start | bytes 196616 | tf_op jit(solution)/shard_map/ppermute | solution.py:143
  311.4 25.7 %collective-permute-start.8 = (bf16[1,128,256]{2,1,0:T(8,128)(2,1)}, bf16[1,128,256]{2,1,0:T(8,128)(2,1)}, u32[]{:S(2)}, u32[]{:S(2)}) collective-permute-start(bf16[1,128,256]{2,1,0:T(8,128)(2,1)} %get-tuple-element.168), channel_id=1, source_target_pairs={{0,1},{1,2},{2,3},{3,4},{4,5},{5,6},{6,7},{8,9},{9,10},{10,11},{11... | collective-permute-start | bytes 196616 | tf_op jit(solution)/shard_map/ppermute | solution.py:144
  313.6 23.6 %collective-permute-start.9 = (bf16[1,128,256]{2,1,0:T(8,128)(2,1)}, bf16[1,128,256]{2,1,0:T(8,128)(2,1)}, u32[]{:S(2)}, u32[]{:S(2)}) collective-permute-start(bf16[1,128,256]{2,1,0:T(8,128)(2,1)} %get-tuple-element.169), channel_id=1, source_target_pairs={{1,0},{2,1},{3,2},{4,3},{5,4},{6,5},{7,6},{9,8},{10,9},{11,10},{12... | collective-permute-start | bytes 196616 | tf_op jit(solution)/shard_map/ppermute | solution.py:143
  372.1 9.3 %collective-permute-start.10 = (f32[1,32,256]{2,1,0:T(8,128)}, f32[1,32,256]{2,1,0:T(8,128)}, u32[]{:S(2)}, u32[]{:S(2)}) collective-permute-start(f32[1,32,256]{2,1,0:T(8,128)} %copy.294), channel_id=1, source_target_pairs={{0,1},{1,2},{2,3},{3,4},{4,5},{5,6},{6,7},{8,9},{9,10},{10,11},{11... | collective-permute-start | bytes 98312 | tf_op jit(solution)/shard_map/ppermute | solution.py:144
  377.8 26.7 %copy-start.13 = (bf16[9,256,256]{2,1,0:T(8,128)(2,1)S(1)}, bf16[9,256,256]{2,1,0:T(8,128)(2,1)}, u32[]{:S(2)}) copy-start(bf16[9,256,256]{2,1,0:T(8,128)(2,1)} %slice.505) | copy-start | bytes 3538948
  377.8 26.7 %copy-start.30 = (bf16[3,3,256,256]{3,2,1,0:T(8,128)(2,1)S(1)}, bf16[3,3,256,256]{3,2,1,0:T(8,128)(2,1)}, u32[]{:S(2)}) copy-start(bf16[3,3,256,256]{3,2,1,0:T(8,128)(2,1)} %fusion.70) | copy-start | bytes 3538948
  380.0 3.8 collective-permute-start.11
  406.6 120.7 %all-gather.11.cloned.1.call-start = ((), (), s32[]{:S(2)}) async-start(), calls=%async_computation.4 | async-start | bytes 2359296 | tf_op jit(solution)/shard_map/all_gather | solution.py:368
  411.8 31.1 %copy-start.77 = (f32[1024]{0:T(1024)S(1)}, f32[1024]{0:T(1024)}, u32[]{:S(2)}) copy-start(f32[1024]{0:T(1024)} %get-tuple-element.196) | copy-start | bytes 12292
  411.8 33.2 %copy-start.130 = (u32[32]{0:T(128)S(1)}, u32[32]{0:T(128)}, u32[]{:S(2)}) copy-start(u32[32]{0:T(128)} %constant.216) | copy-start | bytes 388
  414.3 84.7 %copy-start.54 = (f32[8,256]{1,0:T(8,128)S(1)}, f32[8,256]{1,0:T(8,128)}, u32[]{:S(2)}) copy-start(f32[8,256]{1,0:T(8,128)} %shard_map.311) | copy-start | bytes 24580
  414.3 85.3 %copy-start.15 = (bf16[16,48,128]{2,1,0:T(8,128)(2,1)S(1)}, bf16[16,48,128]{2,1,0:T(8,128)(2,1)}, u32[]{:S(2)}) copy-start(bf16[16,48,128]{2,1,0:T(8,128)(2,1)} %reduce-scatter.8.cloned.1.call-done) | copy-start | bytes 589828
  414.3 85.3 %copy-start.97 = (f32[48]{0:T(128)S(1)}, f32[48]{0:T(128)}, u32[]{:S(2)}) copy-start(f32[48]{0:T(128)} %copy-done.95) | copy-start | bytes 580
  414.3 85.3 %copy-start.100 = (f32[48]{0:T(128)S(1)}, f32[48]{0:T(128)}, u32[]{:S(2)}) copy-start(f32[48]{0:T(128)} %copy-done.98) | copy-start | bytes 580
  414.3 85.3 %copy-start.122 = (f32[48]{0:T(128)S(1)}, f32[48]{0:T(128)}, u32[]{:S(2)}) copy-start(f32[48]{0:T(128)} %get-tuple-element.144) | copy-start | bytes 580
  444.9 134.2 %all-reduce.14.cloned.1.call-start = ((), (), s32[]{:S(2)}) async-start(), calls=%async_computation.7 | async-start | bytes 1572864 | tf_op jit(solution)/shard_map/psum | solution.py:420
  498.9 29.2 %copy-start.94 = (f32[16,128]{1,0:T(8,128)S(1)}, f32[16,128]{1,0:T(8,128)}, u32[]{:S(2)}) copy-start(f32[16,128]{1,0:T(8,128)} %get-tuple-element.230) | copy-start | bytes 24580
  498.9 29.2 %copy-start.105 = (f32[256]{0:T(256)S(1)}, f32[256]{0:T(256)}, u32[]{:S(2)}) copy-start(f32[256]{0:T(256)} %copy-done.104) | copy-start | bytes 3076
  498.9 29.2 %copy-start.107 = (f32[1,256]{1,0:T(1,128)S(1)}, f32[1,256]{1,0:T(1,128)}, u32[]{:S(2)}) copy-start(f32[1,256]{1,0:T(1,128)} %copy-done.106) | copy-start | bytes 3076
  498.9 29.2 %copy-start.127 = (f32[1,256]{1,0:T(1,128)S(1)}, f32[1,256]{1,0:T(1,128)}, u32[]{:S(2)}) copy-start(f32[1,256]{1,0:T(1,128)} %copy-done.126) | copy-start | bytes 3076
  498.9 29.2 %copy-start.129 = (f32[21]{0:T(128)S(1)}, f32[21]{0:T(128)}, u32[]{:S(2)}) copy-start(f32[21]{0:T(128)} %param.35) | copy-start | bytes 256
  498.9 107.5 %all-gather.13.cloned.1.call-start = ((), (), s32[]{:S(2)}) async-start(), calls=%async_computation.5 | async-start | bytes 1769472 | tf_op jit(solution)/shard_map/all_gather | solution.py:382
  501.5 194.2 %all-gather.19.cloned.1.call-start = ((), (), s32[]{:S(2)}) async-start(), calls=%async_computation.9 | async-start | bytes 10485760 | tf_op jit(solution)/shard_map/all_gather | solution.py:369
  527.3 205.7 %all-gather.15.cloned.1.call-start = ((), (), s32[]{:S(2)}) async-start(), calls=%async_computation.6 | async-start | bytes 2621440 | tf_op jit(solution)/shard_map/all_gather | solution.py:370
  530.8 75.6 %copy-start.57 = (bf16[32,48]{1,0:T(8,128)(2,1)S(1)}, bf16[32,48]{1,0:T(8,128)(2,1)}, u32[]{:S(2)}) copy-start(bf16[32,48]{1,0:T(8,128)(2,1)} %param.30) | copy-start | bytes 9220
  736.8 21.6 %copy-start.17 = (bf16[4,32,32,256]{3,2,1,0:T(8,128)(2,1)S(1)}, bf16[4,32,32,256]{3,2,1,0:T(8,128)(2,1)}, u32[]{:S(2)}) copy-start(bf16[4,32,32,256]{3,2,1,0:T(8,128)(2,1)} %get-tuple-element.158) | copy-start | bytes 6291460
  736.8 21.6 %copy-start.128 = (bf16[4,32,32,256]{3,2,1,0:T(8,128)(2,1)S(1)}, bf16[4,32,32,256]{3,2,1,0:T(8,128)(2,1)}, u32[]{:S(2)}) copy-start(bf16[4,32,32,256]{3,2,1,0:T(8,128)(2,1)} %all-gather.15.cloned.1.call-done) | copy-start | bytes 6291460
  (88 other events, 519.6 us)
Sparse Core Ops, SparseCore 0:
  11.3 36.8 reduce-scatter.7
  51.1 33.5 reduce-scatter.5
  86.9 40.9 all-gather.16
  406.6 89.5 all-reduce.15
  498.3 28.9 all-gather.10
  530.8 48.2 all-reduce.13
  581.3 25.0 all-gather.12
  608.4 87.2 all-gather.18
  697.7 35.3 all-gather.14
